TPU v7x, 512 devices: a whole 4x8x8 slice. The times are simulated.
512 devices in a mesh: wide: 64 (over x, y_hi, z), narrow: 8 (over y_lo, core).
Axes of the slice: x: 4, y: 8 (y_hi: 2, y_lo: 4; y = y_hi * 4 + y_lo), z: 8, core: 2. Of those that a mesh axis runs over, the one named last changes fastest.
Arguments:
- query_rows: bfloat16 [65536, 512], P(('wide', 'narrow')), may hold values from -6 to 6
- key_rows: bfloat16 [65536, 512], P(('wide', 'narrow')), may hold values from -6 to 6
- value_rows: bfloat16 [65536, 512], P(('wide', 'narrow')), may hold values from -6 to 6
- out_grad: bfloat16 [65536, 512], P(('wide', 'narrow')), may hold values from -6 to 6
- doc_lengths: int32 [1024], replicated, may hold values from 1 to 40960, 65536 in all
- projection: float32 [128, 64], replicated, may hold values from -6 to 6
Outputs:
- attended: bfloat16 [65536, 512], P(('wide', 'narrow'))
- query_grad: bfloat16 [65536, 512], P(('wide', 'narrow'))
- key_grad: bfloat16 [65536, 512], P(('wide', 'narrow'))
- value_grad: bfloat16 [65536, 512], P(('wide', 'narrow'))
Inputs may be any that keep to these rules, and one draw needn't show every extreme that they name: `doc_lengths`: positive document lengths that sum to 65536; the longest is exactly 40960.
All inputs are finite; a program needn't handle non-finite values.
Results may differ from a plain program's by a relative error of at most 0.0053.
Values may be sent and summed in bfloat16 or wider, within the bound.
A program may use at most 128 MiB of HBM per device.

v0:
```python
import math

import jax
import jax.numpy as jnp
from jax import lax
from jax.sharding import PartitionSpec as P

HEAD_DIM = 64
FEATURES = 128


HIGHEST_PRECISION = lax.Precision.HIGHEST
feature_floor = 1e-06


def positive_features(scaled, projection):
    mixed = jnp.einsum("hre,me->hrm", scaled, projection, precision=HIGHEST_PRECISION)
    half_norm = 0.5 * jnp.sum(scaled * scaled, axis=-1, keepdims=True)
    factor = 1.0 / math.sqrt(FEATURES)
    exponent = jnp.exp(mixed - half_norm) * factor
    return (exponent, (exponent + feature_floor * factor).astype(jnp.bfloat16))


def feature_grad(scaled, exponent, upstream, projection):
    weighted = exponent * upstream
    back_proj = jnp.einsum("hrm,me->hre", weighted, projection, precision=HIGHEST_PRECISION)
    return (back_proj - scaled * jnp.sum(weighted, axis=-1, keepdims=True)) * HEAD_DIM ** (-0.25)


def masked_state(weights, features, vectors):
    return jnp.einsum(
        "hrm,hre->hme", features * weights[None, :, None], vectors, precision=HIGHEST_PRECISION
    )


def masked_total(weights, features):
    return jnp.einsum("r,hrm->hm", weights, features, precision=HIGHEST_PRECISION)


def masked_bias_total(weights, features, biases):
    return jnp.einsum(
        "hr,hrm->hm", biases * weights[None, :], features, precision=HIGHEST_PRECISION
    )


def widen(flag, target):
    return flag.reshape(flag.shape + (1,) * (target.ndim - flag.ndim))


def combine_pieces(earlier, later):
    keep_state = widen(later[2], later[0]) > 0
    keep_total = widen(later[2], later[1]) > 0
    return (
        jnp.where(keep_state, later[0], earlier[0] + later[0]),
        jnp.where(keep_total, later[1], earlier[1] + later[1]),
        jnp.maximum(earlier[2], later[2]),
    )


def pick_entry(table, index, valid):
    return tuple(
        (lax.dynamic_index_in_dim(part, index, 0, keepdims=False) * valid for part in table[:2])
    )


def document_chains(back_piece, front_piece):
    table = (
        lax.all_gather(back_piece[0][None], "wide", axis=0, tiled=True),
        lax.all_gather(back_piece[1][None], "wide", axis=0, tiled=True),
        lax.all_gather(front_piece[0][None], "wide", axis=0, tiled=True),
        lax.all_gather(front_piece[1][None], "wide", axis=0, tiled=True),
        lax.all_gather(back_piece[2][None], "wide", axis=0, tiled=True),
    )
    count = table[0].shape[0]
    place = lax.axis_index("wide")
    rising = lax.associative_scan(combine_pieces, (table[0], table[1], table[4]))
    falling = lax.associative_scan(combine_pieces, (table[2], table[3], table[4]), reverse=True)
    before = pick_entry(rising, jnp.maximum(place - 1, 0), (place > 0).astype(jnp.float32))
    after = pick_entry(
        falling, jnp.minimum(place + 1, count - 1), (place < count - 1).astype(jnp.float32)
    )
    return (before, after)


def tile_chains(back_states, back_totals, front_states, front_totals, tile_reset, before, after):
    zero_flag = jnp.zeros((1, 1), jnp.float32)
    rising = lax.associative_scan(
        combine_pieces,
        (
            jnp.concatenate([before[0][None], back_states], 0),
            jnp.concatenate([before[1][None], back_totals], 0),
            jnp.concatenate([zero_flag, tile_reset], 0),
        ),
    )
    falling = lax.associative_scan(
        combine_pieces,
        (
            jnp.concatenate([front_states, after[0][None]], 0),
            jnp.concatenate([front_totals, after[1][None]], 0),
            jnp.concatenate([tile_reset, zero_flag], 0),
        ),
        reverse=True,
    )
    count = back_states.shape[0]
    return ((rising[0][:count], rising[1][:count]), (falling[0][1:], falling[1][1:]))


def body(query_rows, key_rows, value_rows, out_grad, doc_lengths, projection):
    tok_rows = query_rows.shape[0]
    heads_all = query_rows.shape[1] // HEAD_DIM

    def heads_view(matrix):
        return matrix.reshape(tok_rows, heads_all, HEAD_DIM)

    moved = (
        lax.all_to_all(heads_view(query_rows), "narrow", split_axis=1, concat_axis=0, tiled=True),
        lax.all_to_all(heads_view(key_rows), "narrow", split_axis=1, concat_axis=0, tiled=True),
        lax.all_to_all(heads_view(value_rows), "narrow", split_axis=1, concat_axis=0, tiled=True),
        lax.all_to_all(heads_view(out_grad), "narrow", split_axis=1, concat_axis=0, tiled=True),
    )
    rows = moved[0].shape[0]

    def as_heads(tensor):
        return jnp.transpose(tensor, (1, 0, 2)).astype(jnp.float32)

    first_row = lax.axis_index("wide") * rows
    starts = jnp.cumsum(doc_lengths) - doc_lengths
    positions = first_row + jnp.arange(rows, dtype=jnp.int32)
    doc_ids = jnp.searchsorted(starts, positions, side="right") - 1
    opens = (starts[doc_ids] == positions).astype(jnp.float32)
    front_use = (doc_ids == doc_ids[0]).astype(jnp.float32) * (1.0 - opens[0])
    back_use = (doc_ids == doc_ids[rows - 1]).astype(jnp.float32)
    reset = jnp.max(opens).reshape(1)
    inv_root = HEAD_DIM ** (-0.25)
    query_scaled = as_heads(moved[0]) * inv_root
    key_scaled = as_heads(moved[1]) * inv_root
    value_heads = as_heads(moved[2])
    grad_heads = as_heads(moved[3])
    query_exp, query_bf = positive_features(query_scaled, projection)
    key_exp, key_bf = positive_features(key_scaled, projection)
    query_phi = query_bf.astype(jnp.float32)
    key_phi = key_bf.astype(jnp.float32)
    local_heads = query_phi.shape[0]
    back_piece = (
        masked_state(back_use, key_phi, value_heads),
        masked_total(back_use, key_phi),
        reset,
    )
    front_piece = (
        masked_state(front_use, key_phi, value_heads),
        masked_total(front_use, key_phi),
        reset,
    )
    before, after = document_chains(back_piece, front_piece)
    tile = 128
    count = rows // tile

    def tiles(tensor):
        return tensor.reshape(local_heads, count, tile, tensor.shape[-1])

    def untile(tensor):
        return tensor.reshape(local_heads, rows, tensor.shape[-1])

    ids_tiled = doc_ids.reshape(count, tile)
    opens_tiled = opens.reshape(count, tile)
    tile_front = (ids_tiled == ids_tiled[:, :1]).astype(jnp.float32) * (1.0 - opens_tiled[:, :1])
    tile_back = (ids_tiled == ids_tiled[:, tile - 1 :]).astype(jnp.float32)
    tile_reset = jnp.max(opens_tiled, axis=1, keepdims=True)
    mask = (ids_tiled[:, :, None] == ids_tiled[:, None, :]).astype(jnp.float32)
    front = tile_front[None, :, :, None]
    back = tile_back[None, :, :, None]
    q_tiled = tiles(query_phi)
    k_tiled = tiles(key_phi)
    v_tiled = tiles(value_heads)

    def tile_pieces(weights, features, vectors):
        return jnp.einsum(
            "hnsm,ns,hnse->nhme", features, weights, vectors, precision=HIGHEST_PRECISION
        )

    def tile_totals(weights, features):
        return jnp.einsum("hnsm,ns->nhm", features, weights, precision=HIGHEST_PRECISION)

    def flip(total):
        return jnp.transpose(total, (1, 0, 2))[:, :, None, :]

    pre_part, post_part = tile_chains(
        tile_pieces(tile_back, k_tiled, v_tiled),
        tile_totals(tile_back, k_tiled),
        tile_pieces(tile_front, k_tiled, v_tiled),
        tile_totals(tile_front, k_tiled),
        tile_reset,
        before,
        after,
    )
    scores = (
        jnp.einsum(
            "hnrm,hnsm->hnrs", tiles(query_bf), tiles(key_bf), preferred_element_type=jnp.float32
        )
        * mask[None]
    )
    numer = jnp.einsum("hnrs,hnse->hnre", scores, v_tiled, precision=HIGHEST_PRECISION)
    numer = numer + front * jnp.einsum(
        "hnrm,nhme->hnre", q_tiled, pre_part[0], precision=HIGHEST_PRECISION
    )
    numer = numer + back * jnp.einsum(
        "hnrm,nhme->hnre", q_tiled, post_part[0], precision=HIGHEST_PRECISION
    )
    denom_t = jnp.sum(scores, axis=-1)
    denom_t = denom_t + front[..., 0] * jnp.einsum(
        "hnrm,nhm->hnr", q_tiled, pre_part[1], precision=HIGHEST_PRECISION
    )
    denom_t = denom_t + back[..., 0] * jnp.einsum(
        "hnrm,nhm->hnr", q_tiled, post_part[1], precision=HIGHEST_PRECISION
    )
    attended_f = untile(numer / denom_t[..., None])
    denom = denom_t.reshape(local_heads, rows)
    scaled_grad = grad_heads / denom[..., None]
    bias_term = -jnp.sum(grad_heads * attended_f, axis=-1) / denom
    grad_back = (
        masked_state(back_use, query_phi, scaled_grad),
        masked_bias_total(back_use, query_phi, bias_term),
        reset,
    )
    grad_front = (
        masked_state(front_use, query_phi, scaled_grad),
        masked_bias_total(front_use, query_phi, bias_term),
        reset,
    )
    grad_before, grad_after = document_chains(grad_back, grad_front)
    sg_tiled = tiles(scaled_grad)
    bias_tiled = bias_term.reshape(local_heads, count, tile)

    def grad_totals(weights):
        return jnp.einsum(
            "hnrm,nr,hnr->nhm", q_tiled, weights, bias_tiled, precision=HIGHEST_PRECISION
        )

    gpre, gpost = tile_chains(
        tile_pieces(tile_back, q_tiled, sg_tiled),
        grad_totals(tile_back),
        tile_pieces(tile_front, q_tiled, sg_tiled),
        grad_totals(tile_front),
        tile_reset,
        grad_before,
        grad_after,
    )
    coupling = (
        jnp.einsum("hnre,hnse->hnrs", sg_tiled, v_tiled, precision=HIGHEST_PRECISION)
        + bias_tiled[..., None]
    ) * mask[None]
    query_up = jnp.einsum("hnrs,hnsm->hnrm", coupling, k_tiled, precision=HIGHEST_PRECISION)
    query_up = query_up + front * (
        jnp.einsum("nhme,hnre->hnrm", pre_part[0], sg_tiled, precision=HIGHEST_PRECISION)
        + bias_tiled[..., None] * flip(pre_part[1])
    )
    query_up = query_up + back * (
        jnp.einsum("nhme,hnre->hnrm", post_part[0], sg_tiled, precision=HIGHEST_PRECISION)
        + bias_tiled[..., None] * flip(post_part[1])
    )
    key_up = jnp.einsum("hnrs,hnrm->hnsm", coupling, q_tiled, precision=HIGHEST_PRECISION)
    key_up = key_up + front * (
        jnp.einsum("nhme,hnse->hnsm", gpre[0], v_tiled, precision=HIGHEST_PRECISION) + flip(gpre[1])
    )
    key_up = key_up + back * (
        jnp.einsum("nhme,hnse->hnsm", gpost[0], v_tiled, precision=HIGHEST_PRECISION)
        + flip(gpost[1])
    )
    value_up = jnp.einsum("hnrs,hnre->hnse", scores, sg_tiled, precision=HIGHEST_PRECISION)
    value_up = value_up + front * jnp.einsum(
        "nhme,hnsm->hnse", gpre[0], k_tiled, precision=HIGHEST_PRECISION
    )
    value_up = value_up + back * jnp.einsum(
        "nhme,hnsm->hnse", gpost[0], k_tiled, precision=HIGHEST_PRECISION
    )
    query_out = feature_grad(query_scaled, query_exp, untile(query_up), projection)
    key_out = feature_grad(key_scaled, key_exp, untile(key_up), projection)

    def token_view(tensor):
        return jnp.transpose(tensor, (1, 0, 2)).astype(jnp.bfloat16)

    results = (
        lax.all_to_all(token_view(attended_f), "narrow", split_axis=0, concat_axis=1, tiled=True),
        lax.all_to_all(token_view(query_out), "narrow", split_axis=0, concat_axis=1, tiled=True),
        lax.all_to_all(token_view(key_out), "narrow", split_axis=0, concat_axis=1, tiled=True),
        lax.all_to_all(
            token_view(untile(value_up)), "narrow", split_axis=0, concat_axis=1, tiled=True
        ),
    )
    width = heads_all * HEAD_DIM
    return (
        results[0].reshape(tok_rows, width),
        results[1].reshape(tok_rows, width),
        results[2].reshape(tok_rows, width),
        results[3].reshape(tok_rows, width),
    )


def solution(mesh):
    in_specs = (
        P(("wide", "narrow"), None),
        P(("wide", "narrow"), None),
        P(("wide", "narrow"), None),
        P(("wide", "narrow"), None),
        P(),
        P(),
    )
    out_specs = (
        P(("wide", "narrow"), None),
        P(("wide", "narrow"), None),
        P(("wide", "narrow"), None),
        P(("wide", "narrow"), None),
    )
    return jax.shard_map(body, mesh=mesh, in_specs=in_specs, out_specs=out_specs, check_vma=False)
```

profile of v0, /device:TPU:1, one launch (start us, length us, event | category | flops | bytes accessed | tf_op | source)
XLA Modules:
  0.0 2024.5 jit_solution(9745520373953942066)
XLA Ops:
  8.8 10.2 all-to-all-start.1
  20.9 50.7 %while.24 = (s32[]{:T(128)}, u32[1024]{0:T(1024)S(1)}, u32[1024]{0:T(1024)S(1)}, s32[1024]{0:T(1024)S(1)}, s32[]{:T(128)}, /*index=5*/s32[]{:T(128)}, s32[]{:T(128)}, s32[]{}) while((s32[]{:T(128)}, u32[1024]{0:T(1024)S(1)}, u32[1024]{0:T(1024)S(1)}, s32[1024]{0:T(1024)S(1)}, s32[]{:T(128)}, /*index=5*/s32[]{:T(128)}, s32[]{:T(128)}, ...), condition=%wide.region_3.4_spmd.clone, body=%wide.region_2.3_spmd.clone.sunk | while | flops 20484 | bytes 63601 | solution.py:129
  25.6 4.5 gather_fusion
  30.2 4.5 gather_fusion
  34.8 4.5 gather_fusion
  39.4 4.5 gather_fusion
  44.0 4.5 gather_fusion
  48.6 4.5 gather_fusion
  53.2 4.5 gather_fusion
  57.8 4.5 gather_fusion
  62.4 4.5 gather_fusion
  67.1 4.5 gather_fusion
  79.6 198.3 %all-reduce.144 = f32[64]{0:T(128)S(1)} all-reduce(f32[64]{0:T(128)S(1)} %dynamic-update-slice), channel_id=1, replica_groups=mesh['wide'=64,'narrow'=8] {'wide'}, use_global_device_ids=true, to_apply=%add.144 | all-reduce | flops 64 | bytes 512
  297.7 32.9 %all-to-all-start = ((bf16[128,8,64]{0,2,1:T(8,128)(2,1)}), bf16[128,8,64]{0,2,1:T(8,128)(2,1)S(1)}, u32[]{:S(2)}, u32[]{:S(2)}) async-start(bf16[128,8,64]{0,2,1:T(8,128)(2,1)} %bitcast.3), calls=%async_computation | async-start | bytes 262144 | tf_op jit(solution)/shard_map/all_to_all | solution.py:116
  333.6 183.7 %all-gather.9 = f32[64,1,128]{2,1,0:T(1,128)S(1)} all-gather(f32[1,1,128]{2,1,0:T(1,128)S(1)} %convolution_bitcast_fusion.6), channel_id=5, replica_groups=mesh['wide'=64,'narrow'=8] {'wide'}, dimensions={0}, use_global_device_ids=true | all-gather | bytes 33280 | tf_op jit(solution)/shard_map/all_gather | solution.py:71
  520.9 185.2 %all-gather.8 = f32[64,1,128]{2,1,0:T(1,128)S(1)} all-gather(f32[1,1,128]{2,1,0:T(1,128)S(1)} %convolution_bitcast_fusion.7), channel_id=4, replica_groups=mesh['wide'=64,'narrow'=8] {'wide'}, dimensions={0}, use_global_device_ids=true | all-gather | bytes 33280 | tf_op jit(solution)/shard_map/all_gather | solution.py:69
  708.9 61.3 %all-to-all-start.4 = ((bf16[128,8,64]{0,2,1:T(8,128)(2,1)}), bf16[128,8,64]{0,2,1:T(8,128)(2,1)S(1)}, u32[]{:S(2)}, u32[]{:S(2)}) async-start(bf16[128,8,64]{0,2,1:T(8,128)(2,1)} %bitcast.99), calls=%async_computation.4 | async-start | bytes 262144 | tf_op jit(solution)/shard_map/all_to_all | solution.py:119
  770.6 5.4 all-to-all-done.4
  782.8 9.4 all_to_all.102
  801.9 91.3 %all-gather.23.cloned.1.call-done = f32[8192,64]{0,1:T(8,128)} async-done(((f32[128,64]{0,1:T(8,128)}), f32[8192,64]{0,1:T(8,128)}) %all-gather.23.cloned.1.call-update) | async-done | bytes 2097168 | tf_op jit(solution)/shard_map/all_gather | solution.py:70
  905.5 114.6 %all-gather.21.cloned.1.call-done = f32[8192,64]{0,1:T(8,128)} async-done(((f32[128,64]{0,1:T(8,128)}), f32[8192,64]{0,1:T(8,128)}) %all-gather.21.cloned.1.call-update) | async-done | bytes 2097168 | tf_op jit(solution)/shard_map/all_gather | solution.py:68
  1032.5 114.6 %all-gather.19.cloned.1.call-done = f32[8192,64]{0,1:T(8,128)} async-done(((f32[128,64]{0,1:T(8,128)}), f32[8192,64]{0,1:T(8,128)}) %all-gather.19.cloned.1.call-update) | async-done | bytes 2097168 | tf_op jit(solution)/shard_map/all_gather | solution.py:70
  1213.5 5.1 pad.562
  1218.6 5.1 pad.563
  1223.7 5.2 pad.473
  1235.9 6.2 pad.564
  1242.1 9.2 pad.565
  1251.3 5.9 pad.475
  1264.3 12.4 pad.476
  1279.7 16.6 pad.566
  1296.4 16.7 pad.567
  1320.4 16.6 pad.477
  1361.7 4.5 add_select_fusion.1
  1412.9 5.1 pad.526
  1418.0 5.1 pad.527
  1423.1 5.1 pad.455
  1434.6 6.2 pad.528
  1440.8 9.2 pad.529
  1450.0 5.9 pad.457
  1464.0 11.2 pad.458
  1476.1 11.2 pad.530
  1487.3 11.1 pad.531
  1498.5 11.3 pad.459
  1517.3 187.2 %all-gather.10 = f32[64,1,128]{2,1,0:T(1,128)S(1)} all-gather(f32[1,1,128]{2,1,0:T(1,128)S(1)} %convolution_bitcast_fusion.5), channel_id=7, replica_groups=mesh['wide'=64,'narrow'=8] {'wide'}, dimensions={0}, use_global_device_ids=true | all-gather | bytes 33280 | tf_op jit(solution)/shard_map/all_gather | solution.py:69
  1707.6 183.7 %all-gather.11 = f32[64,1,128]{2,1,0:T(1,128)S(1)} all-gather(f32[1,1,128]{2,1,0:T(1,128)S(1)} %convolution_bitcast_fusion.4), channel_id=9, replica_groups=mesh['wide'=64,'narrow'=8] {'wide'}, dimensions={0}, use_global_device_ids=true | all-gather | bytes 33280 | tf_op jit(solution)/shard_map/all_gather | solution.py:71
  1904.7 68.0 %all-to-all-start.3 = ((bf16[8,2,4096]{2,1,0:T(2,128)(2,1)}), bf16[8,2,4096]{2,1,0:T(2,128)(2,1)S(1)}, u32[]{:S(2)}, u32[]{:S(2)}) async-start(bf16[8,2,4096]{2,1,0:T(2,128)(2,1)} %reshape.1472), calls=%async_computation.3 | async-start | bytes 262144 | tf_op jit(solution)/shard_map/all_to_all | solution.py:283
  1985.0 5.1 all-to-all-start.7
  1990.3 5.6 all-to-all-done.7
  (995 shorter events, 313.9 us)
Async XLA Ops:
  7.2 324.4 %copy-start = (f32[128,64]{0,1:T(8,128)S(1)}, f32[128,64]{0,1:T(8,128)}, u32[]{:S(2)}) copy-start(f32[128,64]{0,1:T(8,128)} %param.13) | copy-start | bytes 98308
  8.8 288.9 %all-to-all-start.1 = ((bf16[128,8,64]{0,2,1:T(8,128)(2,1)}), bf16[128,8,64]{0,2,1:T(8,128)(2,1)S(1)}, u32[]{:S(2)}, u32[]{:S(2)}) async-start(bf16[128,8,64]{0,2,1:T(8,128)(2,1)} %bitcast.9), calls=%async_computation.1 | async-start | bytes 262144 | tf_op jit(solution)/shard_map/all_to_all | solution.py:117
  278.2 427.9 %copy-start.98 = (pred[32]{0:T(512)(128)(4,1)}, pred[32]{0:T(512)(128)(4,1)S(1)}, u32[]{:S(2)}) copy-start(pred[32]{0:T(512)(128)(4,1)S(1)} %compare_bitcast_fusion.22) | copy-start | bytes 100
  278.4 884.9 %copy-start.90 = (pred[32]{0:T(512)(128)(4,1)}, pred[32]{0:T(512)(128)(4,1)S(1)}, u32[]{:S(2)}) copy-start(pred[32]{0:T(512)(128)(4,1)S(1)} %compare_bitcast_fusion.10) | copy-start | bytes 100
  278.7 239.1 %copy-start.145 = (pred[16]{0:T(512)(128)(4,1)}, pred[16]{0:T(512)(128)(4,1)S(1)}, u32[]{:S(2)}) copy-start(pred[16]{0:T(512)(128)(4,1)S(1)} %compare_bitcast_fusion.8) | copy-start | bytes 52
  279.1 887.4 %copy-start.107 = (pred[8]{0:T(512)(128)(4,1)}, pred[8]{0:T(512)(128)(4,1)S(1)}, u32[]{:S(2)}) copy-start(pred[8]{0:T(512)(128)(4,1)S(1)} %compare_bitcast_fusion.6) | copy-start | bytes 28
  279.7 426.5 %copy-start.148 = (pred[16]{0:T(512)(128)(4,1)}, pred[16]{0:T(512)(128)(4,1)S(1)}, u32[]{:S(2)}) copy-start(pred[16]{0:T(512)(128)(4,1)S(1)} %compare_bitcast_fusion.20) | copy-start | bytes 52
  280.0 426.3 %copy-start.117 = (pred[8]{0:T(512)(128)(4,1)}, pred[8]{0:T(512)(128)(4,1)S(1)}, u32[]{:S(2)}) copy-start(pred[8]{0:T(512)(128)(4,1)S(1)} %compare_bitcast_fusion.18) | copy-start | bytes 28
  281.9 498.2 %copy-start.86 = (s32[8]{0:T(128)}, s32[8]{0:T(128)S(1)}, u32[]{:S(2)}) copy-start(s32[8]{0:T(128)S(1)} %get-tuple-element.108) | copy-start | bytes 100
  282.5 497.6 %copy-start.88 = (f32[8]{0:T(128)}, f32[8]{0:T(128)S(1)}, u32[]{:S(2)}) copy-start(f32[8]{0:T(128)S(1)} %subtract_reduce_fusion) | copy-start | bytes 100
  282.5 426.3 %copy-start.137 = (pred[4]{0:T(512)(128)(4,1)}, pred[4]{0:T(512)(128)(4,1)S(1)}, u32[]{:S(2)}) copy-start(pred[4]{0:T(512)(128)(4,1)S(1)} %compare_bitcast_fusion.13) | copy-start | bytes 16
  282.6 237.5 %copy-start.92 = (pred[15]{0:T(512)(128)(4,1)}, pred[15]{0:T(512)(128)(4,1)S(1)}, u32[]{:S(2)}) copy-start(pred[15]{0:T(512)(128)(4,1)S(1)} %compare_bitcast_fusion.9) | copy-start | bytes 49
  282.6 237.5 %copy-start.151 = (pred[7]{0:T(512)(128)(4,1)}, pred[7]{0:T(512)(128)(4,1)S(1)}, u32[]{:S(2)}) copy-start(pred[7]{0:T(512)(128)(4,1)S(1)} %compare_bitcast_fusion.7) | copy-start | bytes 25
  282.8 885.2 %copy-start.112 = (pred[2]{0:T(512)(128)(4,1)}, pred[2]{0:T(512)(128)(4,1)S(1)}, u32[]{:S(2)}) copy-start(pred[2]{0:T(512)(128)(4,1)S(1)} %compare_bitcast_fusion.3) | copy-start | bytes 10
  282.8 424.4 %copy-start.104 = (pred[15]{0:T(512)(128)(4,1)}, pred[15]{0:T(512)(128)(4,1)S(1)}, u32[]{:S(2)}) copy-start(pred[15]{0:T(512)(128)(4,1)S(1)} %compare_bitcast_fusion.21) | copy-start | bytes 49
  282.8 424.1 %copy-start.153 = (pred[7]{0:T(512)(128)(4,1)}, pred[7]{0:T(512)(128)(4,1)S(1)}, u32[]{:S(2)}) copy-start(pred[7]{0:T(512)(128)(4,1)S(1)} %compare_bitcast_fusion.19) | copy-start | bytes 25
  282.8 423.6 %copy-start.142 = (pred[4]{0:T(512)(128)(4,1)}, pred[4]{0:T(512)(128)(4,1)S(1)}, u32[]{:S(2)}) copy-start(pred[4]{0:T(512)(128)(4,1)S(1)} %compare_bitcast_fusion.16) | copy-start | bytes 16
  282.9 423.8 %copy-start.140 = (pred[3]{0:T(512)(128)(4,1)}, pred[3]{0:T(512)(128)(4,1)S(1)}, u32[]{:S(2)}) copy-start(pred[3]{0:T(512)(128)(4,1)S(1)} %compare_bitcast_fusion.17) | copy-start | bytes 13
  283.0 423.5 %copy-start.120 = (pred[2]{0:T(512)(128)(4,1)}, pred[2]{0:T(512)(128)(4,1)S(1)}, u32[]{:S(2)}) copy-start(pred[2]{0:T(512)(128)(4,1)S(1)} %compare_bitcast_fusion.15) | copy-start | bytes 10
  283.0 424.8 %copy-start.101 = (pred[31]{0:T(512)(128)(4,1)}, pred[31]{0:T(512)(128)(4,1)S(1)}, u32[]{:S(2)}) copy-start(pred[31]{0:T(512)(128)(4,1)S(1)} %compare_bitcast_fusion.23) | copy-start | bytes 97
  283.1 493.6 %copy-start.126 = (pred[4]{0:T(512)(128)(4,1)}, pred[4]{0:T(512)(128)(4,1)S(1)}, u32[]{:S(2)}) copy-start(pred[4]{0:T(512)(128)(4,1)S(1)} %compare_bitcast_fusion.14) | copy-start | bytes 16
  283.3 493.2 %copy-start.114 = (pred[2]{0:T(512)(128)(4,1)}, pred[2]{0:T(512)(128)(4,1)S(1)}, u32[]{:S(2)}) copy-start(pred[2]{0:T(512)(128)(4,1)S(1)} %compare_bitcast_fusion.12) | copy-start | bytes 10
  283.5 425.2 %copy-start.129 = (pred[4]{0:T(512)(128)(4,1)}, pred[4]{0:T(512)(128)(4,1)S(1)}, u32[]{:S(2)}) copy-start(pred[4]{0:T(512)(128)(4,1)S(1)} %compare_bitcast_fusion.1) | copy-start | bytes 16
  283.6 492.8 %copy-start.123 = (pred[4]{0:T(512)(128)(4,1)}, pred[4]{0:T(512)(128)(4,1)S(1)}, u32[]{:S(2)}) copy-start(pred[4]{0:T(512)(128)(4,1)S(1)} %compare_bitcast_fusion.2) | copy-start | bytes 16
  285.8 490.4 %copy-start.109 = (pred[2]{0:T(512)(128)(4,1)}, pred[2]{0:T(512)(128)(4,1)S(1)}, u32[]{:S(2)}) copy-start(pred[2]{0:T(512)(128)(4,1)S(1)} %compare_bitcast_fusion) | copy-start | bytes 10
  297.7 482.4 %copy-start.76 = (pred[8,128]{1,0:T(8,128)(4,1)}, pred[8,128]{1,0:T(8,128)(4,1)S(1)}, u32[]{:S(2)}) copy-start(pred[8,128]{1,0:T(8,128)(4,1)S(1)} %get-tuple-element.150) | copy-start | bytes 3076
  297.7 411.2 %all-to-all-start = ((bf16[128,8,64]{0,2,1:T(8,128)(2,1)}), bf16[128,8,64]{0,2,1:T(8,128)(2,1)S(1)}, u32[]{:S(2)}, u32[]{:S(2)}) async-start(bf16[128,8,64]{0,2,1:T(8,128)(2,1)} %bitcast.3), calls=%async_computation | async-start | bytes 262144 | tf_op jit(solution)/shard_map/all_to_all | solution.py:116
  708.9 67.1 %all-to-all-start.4 = ((bf16[128,8,64]{0,2,1:T(8,128)(2,1)}), bf16[128,8,64]{0,2,1:T(8,128)(2,1)S(1)}, u32[]{:S(2)}, u32[]{:S(2)}) async-start(bf16[128,8,64]{0,2,1:T(8,128)(2,1)} %bitcast.99), calls=%async_computation.4 | async-start | bytes 262144 | tf_op jit(solution)/shard_map/all_to_all | solution.py:119
  770.2 122.9 %all-gather.23.cloned.1.call-start = ((), (), s32[]{:S(2)}) async-start(), calls=%async_computation.11 | async-start | bytes 2129920 | tf_op jit(solution)/shard_map/all_gather | solution.py:70
  781.4 238.7 %all-gather.21.cloned.1.call-start = ((), (), s32[]{:S(2)}) async-start(), calls=%async_computation.10 | async-start | bytes 2129920 | tf_op jit(solution)/shard_map/all_gather | solution.py:68
  782.6 364.5 %all-gather.19.cloned.1.call-start = ((), (), s32[]{:S(2)}) async-start(), calls=%async_computation.9 | async-start | bytes 2129920 | tf_op jit(solution)/shard_map/all_gather | solution.py:70
  793.4 555.8 %all-gather.17.cloned.1.call-start = ((), (), s32[]{:S(2)}) async-start(), calls=%async_computation.8 | async-start | bytes 2129920 | tf_op jit(solution)/shard_map/all_gather | solution.py:68
  1513.9 377.5 %copy-start.91 = (pred[32]{0:T(512)(128)(4,1)S(1)}, pred[32]{0:T(512)(128)(4,1)}, u32[]{:S(2)}) copy-start(pred[32]{0:T(512)(128)(4,1)} %copy-done.90) | copy-start | bytes 100
  1513.9 377.7 %copy-start.147 = (pred[16]{0:T(512)(128)(4,1)S(1)}, pred[16]{0:T(512)(128)(4,1)}, u32[]{:S(2)}) copy-start(pred[16]{0:T(512)(128)(4,1)} %copy-done.145) | copy-start | bytes 52
  1513.9 377.8 %copy-start.108 = (pred[8]{0:T(512)(128)(4,1)S(1)}, pred[8]{0:T(512)(128)(4,1)}, u32[]{:S(2)}) copy-start(pred[8]{0:T(512)(128)(4,1)} %copy-done.107) | copy-start | bytes 28
  1513.9 377.8 %copy-start.136 = (pred[4]{0:T(512)(128)(4,1)S(1)}, pred[4]{0:T(512)(128)(4,1)}, u32[]{:S(2)}) copy-start(pred[4]{0:T(512)(128)(4,1)} %copy-done.134) | copy-start | bytes 16
  1513.9 377.9 %copy-start.113 = (pred[2]{0:T(512)(128)(4,1)S(1)}, pred[2]{0:T(512)(128)(4,1)}, u32[]{:S(2)}) copy-start(pred[2]{0:T(512)(128)(4,1)} %copy-done.112) | copy-start | bytes 10
  1514.0 378.3 %copy-start.133 = (pred[3]{0:T(512)(128)(4,1)S(1)}, pred[3]{0:T(512)(128)(4,1)}, u32[]{:S(2)}) copy-start(pred[3]{0:T(512)(128)(4,1)} %copy-done.132) | copy-start | bytes 13
  1514.0 378.5 %copy-start.152 = (pred[7]{0:T(512)(128)(4,1)S(1)}, pred[7]{0:T(512)(128)(4,1)}, u32[]{:S(2)}) copy-start(pred[7]{0:T(512)(128)(4,1)} %copy-done.151) | copy-start | bytes 25
  1514.0 378.8 %copy-start.94 = (pred[15]{0:T(512)(128)(4,1)S(1)}, pred[15]{0:T(512)(128)(4,1)}, u32[]{:S(2)}) copy-start(pred[15]{0:T(512)(128)(4,1)} %copy-done.92) | copy-start | bytes 49
  1514.6 379.0 %copy-start.97 = (pred[31]{0:T(512)(128)(4,1)S(1)}, pred[31]{0:T(512)(128)(4,1)}, u32[]{:S(2)}) copy-start(pred[31]{0:T(512)(128)(4,1)} %copy-done.95) | copy-start | bytes 97
  1514.6 380.2 %copy-start.131 = (pred[4]{0:T(512)(128)(4,1)S(1)}, pred[4]{0:T(512)(128)(4,1)}, u32[]{:S(2)}) copy-start(pred[4]{0:T(512)(128)(4,1)} %copy-done.129) | copy-start | bytes 16
  1514.6 380.3 %copy-start.111 = (pred[2]{0:T(512)(128)(4,1)S(1)}, pred[2]{0:T(512)(128)(4,1)}, u32[]{:S(2)}) copy-start(pred[2]{0:T(512)(128)(4,1)} %copy-done.109) | copy-start | bytes 10
  1516.7 378.8 %copy-start.80 = (f32[8,128]{1,0:T(8,128)}, f32[8,128]{1,0:T(8,128)S(1)}, u32[]{:S(2)}) copy-start(f32[8,128]{1,0:T(8,128)S(1)} %get-tuple-element.126) | copy-start | bytes 12292
  1904.7 80.3 %all-to-all-start.3 = ((bf16[8,2,4096]{2,1,0:T(2,128)(2,1)}), bf16[8,2,4096]{2,1,0:T(2,128)(2,1)S(1)}, u32[]{:S(2)}, u32[]{:S(2)}) async-start(bf16[8,2,4096]{2,1,0:T(2,128)(2,1)} %reshape.1472), calls=%async_computation.3 | async-start | bytes 262144 | tf_op jit(solution)/shard_map/all_to_all | solution.py:283
  1985.0 10.9 all-to-all-start.7
  1995.9 10.1 all-to-all-start.5
  2006.0 10.1 all-to-all-start.6
  (118 other events, 4071.4 us)
Sparse Core Ops, SparseCore 0:
  781.5 111.5 all-gather.22
  898.0 122.0 all-gather.20
  1025.0 122.0 all-gather.18
  1151.3 122.0 all-gather.16
where the time goes:
time: 2050 us; the launch traced here: 2020 us
  blocking collectives  948 us (46%)
  local copies, waits for them, and re-layouts  400 us (20%)
  waiting for transfers between devices  336 us (16%)
  starting transfers between devices  186 us (9%)
  other arithmetic  99.5 us (5%)
  matrix products  30.9 us (2%)
  between operations  23.1 us (1%)
    all_gather x2, blocking collectives, document_chains(): lax.all_gather(back_piece[1][None], 'wide', axis=0, tiled=True)  372 us
    all_gather x2, blocking collectives, document_chains(): lax.all_gather(front_piece[1][None], 'wide', axis=0, tiled=True)  367 us
    all_gather x2, waiting for transfers between devices, document_chains(): lax.all_gather(front_piece[0][None], 'wide', axis=0, tiled=True)  206 us
    unnamed x1, blocking collectives  198 us
    pad x40, local copies, waits for them, and re-layouts, document_chains(): lax.associative_scan(combine_pieces, (table[2], table[3], table[4]), reve...  127 us
    all_gather x2, waiting for transfers between devices, document_chains(): lax.all_gather(back_piece[0][None], 'wide', axis=0, tiled=True)  115 us
    pad x40, local copies, waits for them, and re-layouts, document_chains(): lax.associative_scan(combine_pieces, (table[0], table[1], table[4]))  109 us
    all_to_all x1, starting transfers between devices, body(): lax.all_to_all(token_view(attended_f), 'narrow', split_axis=0, concat_axi...  68 us
  transfers between devices with their start and end apart: 11, of which 7 were waited for; matrix products, arithmetic and copies ran while one was open for 17% of the time, Pallas kernels for 0%

commit v1 on v0

v1 whole, which is shorter than its diff:
```python
import functools

import jax
import jax.numpy as jnp
from jax import lax
from jax.experimental import pallas as pl
from jax.experimental.pallas import tpu as pltpu
from jax.sharding import PartitionSpec as P

HEAD_DIM = 64
FEATURES = 128
LANES = 128
FLOOR = 1e-06
F32 = jnp.float32
BF16 = jnp.bfloat16
INV_ROOT = HEAD_DIM ** (-0.25)
FACTOR = FEATURES ** (-0.5)
VMEM_BYTES = 48 * 1024 * 1024
STRIP = 256


def dot(a, b, da, db):
    return lax.dot_general(a, b, (((da,), (db,)), ((), ())), preferred_element_type=F32)


def split2(x):
    high = x.astype(BF16)
    return high, (x - high.astype(F32)).astype(BF16)


def split3(x):
    high = x.astype(BF16)
    rest = x - high.astype(F32)
    mid = rest.astype(BF16)
    return high, mid, (rest - mid.astype(F32)).astype(BF16)


def dot_exact(a, b, da, db):
    high, low = split2(b)
    return dot(a, high, da, db) + dot(a, low, da, db)


def dot_wide(a, b, da, db):
    a0, a1 = split2(a)
    b0, b1 = split2(b)
    return dot(a0, b0, da, db) + dot(a0, b1, da, db) + dot(a1, b0, da, db)


def features(x, projection):
    parts = split3(projection * INV_ROOT)
    mixed = dot(x, parts[0], 1, 1) + dot(x, parts[1], 1, 1) + dot(x, parts[2], 1, 1)
    wide = x.astype(F32)
    half = jnp.sum(wide * wide, axis=1, keepdims=True) * (0.5 * INV_ROOT * INV_ROOT)
    expo = jnp.exp(mixed - half) * FACTOR
    return expo, (expo + FLOOR * FACTOR).astype(BF16)


def extended(x, extra):
    rows = x.shape[0]
    lane = lax.broadcasted_iota(jnp.int32, (rows, HEAD_DIM), 1)
    tail = jnp.where(lane == 0, jnp.broadcast_to(extra, (rows, HEAD_DIM)), 0.0)
    return jnp.concatenate([x, tail], axis=1)


def feature_grad(x, expo, up, projection):
    weighted = expo * up
    ones = extended(projection, jnp.ones((FEATURES, 1), F32))
    back = dot_wide(weighted, ones, 1, 0)
    scaled = x.astype(F32) * INV_ROOT
    return (back[:, :HEAD_DIM] - scaled * back[:, HEAD_DIM : HEAD_DIM + 1]) * INV_ROOT


def count_ends(ends, positions):
    return jnp.sum(jnp.where(ends <= positions, 1.0, 0.0), axis=1, keepdims=True)


def pack_kernel(q_ref, k_ref, v_ref, g_ref, kv_ref, qg_ref):
    for head in range(kv_ref.shape[0]):
        cols = slice(head * HEAD_DIM, (head + 1) * HEAD_DIM)
        kv_ref[head] = jnp.concatenate([k_ref[:, cols], v_ref[:, cols]], axis=1)
        qg_ref[head] = jnp.concatenate([q_ref[:, cols], g_ref[:, cols]], axis=1)


def unpack_kernel(first_ref, second_ref, out_a, out_b, out_c, out_d):
    for pair in range(first_ref.shape[0] // 2):
        cols = slice(pair * LANES, (pair + 1) * LANES)
        for ref, left, right in ((first_ref, out_a, out_b), (second_ref, out_c, out_d)):
            even, odd = ref[2 * pair], ref[2 * pair + 1]
            left[:, cols] = jnp.concatenate([even[:, :HEAD_DIM], odd[:, :HEAD_DIM]], axis=1)
            right[:, cols] = jnp.concatenate([even[:, HEAD_DIM:], odd[:, HEAD_DIM:]], axis=1)


def store_pieces(ref, back, front):
    owners = ref.shape[0]
    share = FEATURES // owners
    for i in range(share):
        ref[:, i, :] = back[i * owners : (i + 1) * owners]
        ref[:, share + i, :] = front[i * owners : (i + 1) * owners]


def load_pieces(ref):
    owners = ref.shape[0]
    share = FEATURES // owners
    before = jnp.concatenate([ref[:, i, :] for i in range(share)], axis=0)
    after = jnp.concatenate([ref[:, share + i, :] for i in range(share)], axis=0)
    return before, after


def key_kernel(place_ref, ends_ref, kv_ref, proj_ref, piece_ref, phi_ref, expo_ref, ids_ref, row_ref):
    rows = kv_ref.shape[0]
    first = place_ref[0] * rows
    ends = ends_ref[...]
    for strip in range(rows // STRIP):
        at = slice(strip * STRIP, (strip + 1) * STRIP)
        place = lax.broadcasted_iota(jnp.int32, (STRIP, 1), 0) + (first + strip * STRIP)
        ids_ref[at, :] = jnp.broadcast_to(count_ends(ends, place), (STRIP, LANES))
        expo, phi = features(kv_ref[at, :HEAD_DIM], proj_ref[...])
        expo_ref[at, :] = expo
        phi_ref[at, :] = phi
    ids = ids_ref[...]
    row_ref[...] = jnp.transpose(ids)[:8, :]
    front = ids == ids[:1, :]
    back = ids == ids[rows - 1 :, :]
    vectors = extended(kv_ref[:, HEAD_DIM:].astype(F32), jnp.ones((rows, 1), F32))
    both = jnp.concatenate([jnp.where(back, vectors, 0.0), jnp.where(front, vectors, 0.0)], axis=1)
    pieces = dot(phi_ref[...], both.astype(BF16), 0, 0)
    store_pieces(piece_ref, pieces[:, :LANES], pieces[:, LANES:])


def chain_kernel(rows, ends_ref, in_ref, out_ref):
    owners = in_ref.shape[0]
    share = FEATURES // owners
    ends = ends_ref[...]
    block = lax.broadcasted_iota(jnp.int32, (LANES, 1), 0) * rows
    first = jnp.broadcast_to(count_ends(ends, block), (LANES, LANES))
    last = jnp.broadcast_to(count_ends(ends, block + (rows - 1)), (LANES, LANES))
    mine = lax.broadcasted_iota(jnp.int32, (LANES, LANES), 0)
    other = lax.broadcasted_iota(jnp.int32, (LANES, LANES), 1)
    rising = jnp.where((jnp.transpose(last) == first) & (other < mine), 1.0, 0.0)
    falling = jnp.where((jnp.transpose(first) == last) & (other > mine), 1.0, 0.0)
    rising = rising[:owners, :owners].astype(BF16)
    falling = falling[:owners, :owners].astype(BF16)
    for i in range(2 * share):
        chain = rising if i < share else falling
        parts = split3(in_ref[:, i, :])
        out_ref[:, i, :] = dot(chain, parts[0], 1, 0) + dot(chain, parts[1], 1, 0) + dot(chain, parts[2], 1, 0)


def query_kernel(
    kv_ref, qg_ref, proj_ref, phi_k_ref, ids_ref, row_ref, state_ref,
    done_ref, piece_ref, key_up_ref, value_up_ref,
    a_ref, phi_ref,
):
    rows = kv_ref.shape[0]
    before, after = load_pieces(state_ref)
    both = jnp.concatenate([before, after], axis=1)
    both_high, both_low = split2(both)
    phi_k = phi_k_ref[...]
    values = extended(kv_ref[:, HEAD_DIM:].astype(F32), jnp.ones((rows, 1), F32)).astype(BF16)
    id_row = row_ref[:1, :]
    id_first = ids_ref[:1, :]
    id_last = ids_ref[rows - 1 :, :]
    for strip in range(rows // STRIP):
        at = slice(strip * STRIP, (strip + 1) * STRIP)
        ids = ids_ref[at, :]
        front = ids == id_first
        back = ids == id_last
        mask = ids[:, :1] == id_row
        query = qg_ref[at, :HEAD_DIM]
        grad = qg_ref[at, HEAD_DIM:].astype(F32)
        expo, phi = features(query, proj_ref[...])
        phi_ref[at, :] = phi
        scores = jnp.where(mask, dot(phi, phi_k, 1, 1), 0.0)
        score_high, score_low = split2(scores)
        total = dot(score_high, values, 1, 0) + dot(score_low, values, 1, 0)
        far = dot(phi, both_high, 1, 0) + dot(phi, both_low, 1, 0)
        total = total + jnp.where(front, far[:, :LANES], 0.0) + jnp.where(back, far[:, LANES:], 0.0)
        inverse = 1.0 / total[:, HEAD_DIM : HEAD_DIM + 1]
        attended = total[:, :HEAD_DIM] * inverse
        bias = -jnp.sum(grad * attended, axis=1, keepdims=True) * inverse
        a = extended(grad * inverse, bias)
        a_ref[at, :] = a
        a_high, a_low = split2(a)
        coupling = jnp.where(mask, dot(a_high, values, 1, 1) + dot(a_low, values, 1, 1), 0.0)
        coupling_high, coupling_low = split2(coupling)
        up = dot(coupling_high, phi_k, 1, 0) + dot(coupling_low, phi_k, 1, 0)
        up = up + jnp.where(front, dot_wide(a, before, 1, 1), 0.0)
        up = up + jnp.where(back, dot_wide(a, after, 1, 1), 0.0)
        query_grad = feature_grad(query, expo, up, proj_ref[...])
        done_ref[at, :] = jnp.concatenate([attended, query_grad], axis=1).astype(BF16)
        key_up = dot(phi, coupling_high, 0, 0) + dot(phi, coupling_low, 0, 0)
        value_up = dot(a_high, score_high, 0, 0) + dot(a_low, score_high, 0, 0) + dot(a_high, score_low, 0, 0)
        if strip == 0:
            key_up_ref[...] = key_up
            value_up_ref[...] = value_up
        else:
            key_up_ref[...] += key_up
            value_up_ref[...] += value_up
    ids = ids_ref[...]
    a = a_ref[...]
    sides = jnp.concatenate(
        [jnp.where(ids == id_last, a, 0.0), jnp.where(ids == id_first, a, 0.0)], axis=1
    )
    high, low = split2(sides)
    phi = phi_ref[...]
    pieces = dot(phi, high, 0, 0) + dot(phi, low, 0, 0)
    store_pieces(piece_ref, pieces[:, :LANES], pieces[:, LANES:])


def finish_kernel(
    kv_ref, proj_ref, phi_k_ref, expo_ref, ids_ref, state_ref, key_up_ref, value_up_ref, done_ref
):
    rows = kv_ref.shape[0]
    before, after = load_pieces(state_ref)
    both_high, both_low = split2(jnp.concatenate([before, after], axis=1))
    rows_high, rows_low = split2(jnp.concatenate([before, after], axis=0))
    id_first = ids_ref[:1, :]
    id_last = ids_ref[rows - 1 :, :]
    for strip in range(rows // STRIP):
        at = slice(strip * STRIP, (strip + 1) * STRIP)
        ids = ids_ref[at, :]
        front = ids == id_first
        back = ids == id_last
        phi = phi_k_ref[at, :]
        values = extended(kv_ref[at, HEAD_DIM:].astype(F32), jnp.ones((STRIP, 1), F32)).astype(BF16)
        far_key = dot(values, rows_high, 1, 1) + dot(values, rows_low, 1, 1)
        up = jnp.transpose(key_up_ref[:, at])
        up = up + jnp.where(front, far_key[:, :LANES], 0.0) + jnp.where(back, far_key[:, LANES:], 0.0)
        far = dot(phi, both_high, 1, 0) + dot(phi, both_low, 1, 0)
        total = jnp.transpose(value_up_ref[:, at])
        total = total + jnp.where(front, far[:, :LANES], 0.0) + jnp.where(back, far[:, LANES:], 0.0)
        key_grad = feature_grad(kv_ref[at, :HEAD_DIM], expo_ref[at, :], up, proj_ref[...])
        done_ref[at, :] = jnp.concatenate([key_grad, total[:, :HEAD_DIM]], axis=1).astype(BF16)


def call(kernel, outs, operands, flops, scratch=()):
    in_specs = [
        pl.BlockSpec(memory_space=pltpu.SMEM if x.ndim == 1 else pltpu.VMEM) for x in operands
    ]
    moved = sum(x.size * x.dtype.itemsize for x in operands)
    moved += sum(x.size * x.dtype.itemsize for x in outs)
    return pl.pallas_call(
        kernel,
        out_shape=tuple(outs),
        in_specs=in_specs,
        out_specs=tuple(pl.BlockSpec(memory_space=pltpu.VMEM) for _ in outs),
        scratch_shapes=list(scratch),
        compiler_params=pltpu.CompilerParams(vmem_limit_bytes=VMEM_BYTES),
        cost_estimate=pl.CostEstimate(flops=flops, bytes_accessed=moved, transcendentals=0),
    )(*operands)


def exchange(x, axis):
    return lax.all_to_all(x, axis, split_axis=0, concat_axis=0, tiled=True)


def body(coarse, fine, query_rows, key_rows, value_rows, out_grad, doc_lengths, projection):
    own = query_rows.shape[0]
    heads = query_rows.shape[1] // HEAD_DIM
    rows = own * fine
    shape = jax.ShapeDtypeStruct
    packed = shape((heads, own, LANES), BF16)
    place = lax.axis_index("wide").reshape(1).astype(jnp.int32)
    ends = jnp.cumsum(doc_lengths).reshape(1, -1)

    kv, qg = call(pack_kernel, (packed, packed), (query_rows, key_rows, value_rows, out_grad), 0)
    kv = exchange(kv, "narrow").reshape(rows, LANES)
    qg = exchange(qg, "narrow").reshape(rows, LANES)

    pieces = shape((coarse, 2 * FEATURES // coarse, LANES), F32)
    full = shape((rows, LANES), F32)
    turned = shape((LANES, rows), F32)
    piece, phi_k, expo_k, ids, id_row = call(
        key_kernel,
        (pieces, shape((rows, LANES), BF16), full, full, shape((8, rows), F32)),
        (place, ends, kv, projection),
        2 * rows * LANES * LANES * 3,
    )
    chain = functools.partial(chain_kernel, rows)
    (moved,) = call(chain, (pieces,), (ends, exchange(piece, "wide")), 2 * coarse * coarse * 6 * LANES)
    state = exchange(moved, "wide")

    finished = shape((rows, LANES), BF16)
    done_q, piece_g, key_up, value_up = call(
        query_kernel,
        (finished, pieces, turned, turned),
        (kv, qg, projection, phi_k, ids, id_row, state),
        2 * rows * rows * LANES * 12,
        (pltpu.VMEM((rows, LANES), F32), pltpu.VMEM((rows, LANES), BF16)),
    )
    back_q = exchange(done_q.reshape(fine, own, LANES), "narrow")
    (moved_g,) = call(chain, (pieces,), (ends, exchange(piece_g, "wide")), 2 * coarse * coarse * 6 * LANES)
    state_g = exchange(moved_g, "wide")
    (done_k,) = call(
        finish_kernel,
        (finished,),
        (kv, projection, phi_k, expo_k, ids, state_g, key_up, value_up),
        2 * rows * LANES * LANES * 8,
    )
    back_k = exchange(done_k.reshape(fine, own, LANES), "narrow")
    out = shape(query_rows.shape, BF16)
    return call(unpack_kernel, (out, out, out, out), (back_q, back_k), 0)


def solution(mesh):
    tokens = P(("wide", "narrow"), None)
    return jax.shard_map(
        functools.partial(body, mesh.shape["wide"], mesh.shape["narrow"]),
        mesh=mesh,
        in_specs=(tokens, tokens, tokens, tokens, P(), P()),
        out_specs=(tokens, tokens, tokens, tokens),
        check_vma=False,
    )
```

time: 2050 us -> 162 us (0.08); the launches traced: 2020 us -> 162 us
  blocking collectives: 948 us -> 92 us
  local copies, waits for them, and re-layouts: 400 us -> 4.26 us
  waiting for transfers between devices: 336 us -> 23.1 us
  starting transfers between devices: 186 us -> 24.2 us
  other arithmetic: 99.5 us -> 0.38 us
  matrix products: 30.9 us -> 0 us
  between operations: 23.1 us -> 0.69 us
    all_gather x4 -> x0, blocking collectives: 740 us -> none  [the longest x2 372 us: document_chains(): lax.all_gather(back_piece[1][None], 'wide', axis=0, tiled=True)]
    all_gather x4 -> x0, waiting for transfers between devices: 321 us -> none  [the longest x2 206 us: document_chains(): lax.all_gather(front_piece[0][None], 'wide', axis=0, tiled=True)]
    pad x96 -> x0, local copies, waits for them, and re-layouts: 237 us -> none  [the longest x40 127 us: document_chains(): lax.associative_scan(combine_pieces, (table[2], table[3], table[4]), reve...]
    unnamed x1 -> x0, blocking collectives: 198 us -> none
    all_to_all x7 -> x3, starting transfers between devices: 186 us -> 24.2 us  [exchange(): return lax.all_to_all(x, axis, split_axis=0, concat_axis=0, tiled=True)]
    all_to_all x1 -> x5, blocking collectives: 9.4 us -> 92 us  [exchange(): return lax.all_to_all(x, axis, split_axis=0, concat_axis=0, tiled=True)]
    slice x142 -> x1, local copies, waits for them, and re-layouts: 65.1 us -> 0.07 us  [the longest x43 29 us: document_chains(): lax.associative_scan(combine_pieces, (table[2], table[3], table[4]), reve...]
    gather x12 -> x0, local copies, waits for them, and re-layouts: 54.3 us -> none  [the longest x11 49.8 us: body(): doc_ids = jnp.searchsorted(starts, positions, side='right') - 1]
  transfers between devices with their start and end apart: 11 -> 3, of which waited for: 7 -> 3; matrix products, arithmetic and copies ran while one was open for 17% -> 0% of each run, Pallas kernels for 0% -> 1%
where the time goes in v1:
time: 162 us
  blocking collectives  92 us (57%)
  starting transfers between devices  24.2 us (15%)
  waiting for transfers between devices  23.1 us (14%)
  Pallas kernels  17 us (10%)
  local copies, waits for them, and re-layouts  4.26 us (3%)
    all_to_all x5, blocking collectives, exchange(): return lax.all_to_all(x, axis, split_axis=0, concat_axis=0, tiled=True)  92 us
    all_to_all x3, starting transfers between devices, exchange(): return lax.all_to_all(x, axis, split_axis=0, concat_axis=0, tiled=True)  24.2 us
    all_to_all x3, waiting for transfers between devices, exchange(): return lax.all_to_all(x, axis, split_axis=0, concat_axis=0, tiled=True)  23.1 us
    pallas_call x7, Pallas kernels, call(): pl.pallas_call(kernel, out_shape=tuple(outs), in_specs=in_specs, out_spec...  17 us
    unnamed x13, local copies, waits for them, and re-layouts  4.07 us
  transfers between devices with their start and end apart: 3, of which 3 were waited for; matrix products, arithmetic and copies ran while one was open for 0% of the time, Pallas kernels for 1%

profile of v1, /device:TPU:1, one launch (start us, length us, event | category | flops | bytes accessed | tf_op | source)
XLA Modules:
  0.0 161.6 jit_solution(2196381088129385209)
XLA Ops:
  0.6 0.0 copy-start
  0.6 0.9 copy-done
  1.5 0.0 copy-start.1
  1.5 0.9 copy-done.1
  2.4 0.0 copy-start.2
  2.4 0.9 copy-done.2
  3.3 0.0 copy-start.3
  3.3 0.9 copy-done.3
  4.3 1.0 shard_map.93
  5.2 0.0 copy-start.5
  5.2 10.3 %all-to-all-start = ((bf16[8,128,128]{2,1,0:T(8,128)(2,1)}), bf16[8,128,128]{2,1,0:T(8,128)(2,1)S(1)}, u32[]{:S(2)}, u32[]{:S(2)}) async-start(bf16[8,128,128]{2,1,0:T(8,128)(2,1)} %get-tuple-element.15), calls=%async_computation | async-start | bytes 524288 | tf_op jit(solution)/shard_map/all_to_all | solution.py:254
  15.6 0.0 copy-start.4
  15.6 0.0 copy-done.5
  15.6 0.3 reduce-window.9
  15.8 0.1 slice.7
  16.0 0.4 copy-done.4
  16.3 0.1 copy.14.proj_ref
  16.4 0.1 slice_reduce_fusion
  16.5 0.1 broadcast_add_fusion
  16.6 7.7 %all-to-all-done = bf16[8,128,128]{2,1,0:T(8,128)(2,1)S(1)} async-done(((bf16[8,128,128]{2,1,0:T(8,128)(2,1)}), bf16[8,128,128]{2,1,0:T(8,128)(2,1)S(1)}, u32[]{:S(2)}, u32[]{:S(2)}) %all-to-all-start) | async-done | bytes 262176 | tf_op jit(solution)/shard_map/all_to_all | solution.py:254
  24.3 1.1 shard_map.94
  25.4 26.7 %all_to_all.40.in_ref = f32[64,4,128]{2,1,0:T(4,128)S(1)} all-to-all(f32[64,4,128]{2,1,0:T(4,128)S(1)} %get-tuple-element.20), channel_id=1, replica_groups=mesh['wide'=64,'narrow'=8] {'wide'}, dimensions={0} | all-to-all | bytes 262144 | tf_op jit(solution)/shard_map/all_to_all | solution.py:254
  52.1 5.8 %all-to-all-start.1 = ((bf16[8,128,128]{2,1,0:T(8,128)(2,1)}), bf16[8,128,128]{2,1,0:T(8,128)(2,1)S(1)}, u32[]{:S(2)}, u32[]{:S(2)}) async-start(bf16[8,128,128]{2,1,0:T(8,128)(2,1)} %get-tuple-element.16), calls=%async_computation.1 | async-start | bytes 524288 | tf_op jit(solution)/shard_map/all_to_all | solution.py:254
  57.9 0.8 shard_map.95
  58.7 7.9 %all-to-all-done.1 = bf16[8,128,128]{2,1,0:T(8,128)(2,1)S(1)} async-done(((bf16[8,128,128]{2,1,0:T(8,128)(2,1)}), bf16[8,128,128]{2,1,0:T(8,128)(2,1)S(1)}, u32[]{:S(2)}, u32[]{:S(2)}) %all-to-all-start.1) | async-done | bytes 262176 | tf_op jit(solution)/shard_map/all_to_all | solution.py:254
  66.6 17.5 %all_to_all.41.state_ref = f32[64,4,128]{2,1,0:T(4,128)S(1)} all-to-all(f32[64,4,128]{2,1,0:T(4,128)S(1)} %shard_map.95), channel_id=1, replica_groups=mesh['wide'=64,'narrow'=8] {'wide'}, dimensions={0} | all-to-all | bytes 262144 | tf_op jit(solution)/shard_map/all_to_all | solution.py:254
  84.2 11.0 %shard_map.96 = (bf16[1024,128]{1,0:T(8,128)(2,1)}, f32[64,4,128]{2,1,0:T(4,128)S(1)}, f32[128,1024]{1,0:T(8,128)S(1)}, f32[128,1024]{1,0:T(8,128)S(1)}) custom-call(bf16[1024,128]{1,0:T(8,128)(2,1)S(1)} %bitcast.8, bf16[1024,128]{1,0:T(8,128)(2,1)S(1)} %bitcast.11, f32[128,64]{1,0:T(8,128)S(1)} %copy.14.proj_ref, ...), custom_call_target="tpu_custom_call" | custom-call | flops 3221225472 | bytes 2949120 | tf_op jit(solution)/shard_map/pallas_call | solution.py:242
  95.2 17.9 %all_to_all.42.in_ref = f32[64,4,128]{2,1,0:T(4,128)S(1)} all-to-all(f32[64,4,128]{2,1,0:T(4,128)S(1)} %get-tuple-element.23), channel_id=1, replica_groups=mesh['wide'=64,'narrow'=8] {'wide'}, dimensions={0} | all-to-all | bytes 262144 | tf_op jit(solution)/shard_map/all_to_all | solution.py:254
  113.1 0.8 shard_map.97
  113.9 17.7 %all_to_all.43.state_ref = f32[64,4,128]{2,1,0:T(4,128)S(1)} all-to-all(f32[64,4,128]{2,1,0:T(4,128)S(1)} %shard_map.97), channel_id=1, replica_groups=mesh['wide'=64,'narrow'=8] {'wide'}, dimensions={0} | all-to-all | bytes 262144 | tf_op jit(solution)/shard_map/all_to_all | solution.py:254
  131.7 8.1 %all-to-all-start.4 = ((bf16[8,128,128]{2,1,0:T(8,128)(2,1)}), bf16[8,128,128]{2,1,0:T(8,128)(2,1)S(1)}, u32[]{:S(2)}, u32[]{:S(2)}) async-start(bf16[8,128,128]{2,1,0:T(8,128)(2,1)} %bitcast.5), calls=%async_computation.4 | async-start | bytes 524288 | tf_op jit(solution)/shard_map/all_to_all | solution.py:254
  139.7 1.2 shard_map.98
  141.0 7.5 %all-to-all-done.4.first_ref = bf16[8,128,128]{2,1,0:T(8,128)(2,1)S(1)} async-done(((bf16[8,128,128]{2,1,0:T(8,128)(2,1)}), bf16[8,128,128]{2,1,0:T(8,128)(2,1)S(1)}, u32[]{:S(2)}, u32[]{:S(2)}) %all-to-all-start.4) | async-done | bytes 262176 | tf_op jit(solution)/shard_map/all_to_all | solution.py:254
  148.5 12.1 %all_to_all.44.second_ref = bf16[8,128,128]{2,1,0:T(8,128)(2,1)S(1)} all-to-all(bf16[8,128,128]{2,1,0:T(8,128)(2,1)S(1)} %bitcast.10), channel_id=1, replica_groups=mesh['wide'=64,'narrow'=8] {'narrow'}, dimensions={0} | all-to-all | bytes 524288 | tf_op jit(solution)/shard_map/all_to_all | solution.py:254
  160.6 1.0 shard_map.99
  (1 shorter events, 0.0 us)
Async XLA Ops:
  0.6 0.9 copy-start
  1.5 0.9 copy-start.1
  2.4 0.9 copy-start.2
  3.3 0.9 copy-start.3
  5.2 10.3 %copy-start.5 = (s32[1024]{0:T(1024)S(1)}, s32[1024]{0:T(1024)}, u32[]{:S(2)}) copy-start(s32[1024]{0:T(1024)} %param.10) | copy-start | bytes 12292
  5.2 19.0 %all-to-all-start = ((bf16[8,128,128]{2,1,0:T(8,128)(2,1)}), bf16[8,128,128]{2,1,0:T(8,128)(2,1)S(1)}, u32[]{:S(2)}, u32[]{:S(2)}) async-start(bf16[8,128,128]{2,1,0:T(8,128)(2,1)} %get-tuple-element.15), calls=%async_computation | async-start | bytes 524288 | tf_op jit(solution)/shard_map/all_to_all | solution.py:254
  15.6 0.8 copy-start.4
  52.1 14.5 %all-to-all-start.1 = ((bf16[8,128,128]{2,1,0:T(8,128)(2,1)}), bf16[8,128,128]{2,1,0:T(8,128)(2,1)S(1)}, u32[]{:S(2)}, u32[]{:S(2)}) async-start(bf16[8,128,128]{2,1,0:T(8,128)(2,1)} %get-tuple-element.16), calls=%async_computation.1 | async-start | bytes 524288 | tf_op jit(solution)/shard_map/all_to_all | solution.py:254
  131.7 16.8 %all-to-all-start.4 = ((bf16[8,128,128]{2,1,0:T(8,128)(2,1)}), bf16[8,128,128]{2,1,0:T(8,128)(2,1)S(1)}, u32[]{:S(2)}, u32[]{:S(2)}) async-start(bf16[8,128,128]{2,1,0:T(8,128)(2,1)} %bitcast.5), calls=%async_computation.4 | async-start | bytes 524288 | tf_op jit(solution)/shard_map/all_to_all | solution.py:254

commit v2 on v1

v2 whole, which is shorter than its diff:
```python
import functools

import jax
import jax.numpy as jnp
from jax import lax
from jax.experimental import pallas as pl
from jax.experimental.pallas import tpu as pltpu
from jax.sharding import PartitionSpec as P

HEAD_DIM = 64
FEATURES = 128
LANES = 128
FLOOR = 1e-06
F32 = jnp.float32
BF16 = jnp.bfloat16
INV_ROOT = HEAD_DIM ** (-0.25)
FACTOR = FEATURES ** (-0.5)
VMEM_BYTES = 56 * 1024 * 1024
MESH = pl.DeviceIdType.MESH
STRIP = 256


def dot(a, b, da, db):
    return lax.dot_general(a, b, (((da,), (db,)), ((), ())), preferred_element_type=F32)


def split2(x):
    high = x.astype(BF16)
    return high, (x - high.astype(F32)).astype(BF16)


def split3(x):
    high = x.astype(BF16)
    rest = x - high.astype(F32)
    mid = rest.astype(BF16)
    return high, mid, (rest - mid.astype(F32)).astype(BF16)


def beside(*parts):
    return jnp.concatenate(parts, axis=1)


def features(x, parts):
    mixed = dot(beside(x, x, x, jnp.zeros_like(x)), parts, 1, 0)
    wide = x.astype(F32)
    half = jnp.sum(wide * wide, axis=1, keepdims=True) * (0.5 * INV_ROOT * INV_ROOT)
    expo = jnp.exp(mixed - half) * FACTOR
    return expo, (expo + FLOOR * FACTOR).astype(BF16)


def extended(x, extra):
    rows = x.shape[0]
    lane = lax.broadcasted_iota(jnp.int32, (rows, HEAD_DIM), 1)
    tail = jnp.where(lane == 0, jnp.broadcast_to(extra, (rows, HEAD_DIM)), 0.0)
    return jnp.concatenate([x, tail], axis=1)


def feature_grad(x, expo, up, parts):
    high, low = split2(expo * up)
    back = dot(beside(high, low), beside(parts[0], parts[0]), 1, 1) + dot(high, parts[1], 1, 1)
    scaled = x.astype(F32) * INV_ROOT
    return (back[:, :HEAD_DIM] - scaled * back[:, HEAD_DIM : HEAD_DIM + 1]) * INV_ROOT


def unpack_kernel(first_ref, second_ref, out_a, out_b, out_c, out_d):
    for pair in range(first_ref.shape[0] // 2):
        cols = slice(pair * LANES, (pair + 1) * LANES)
        for ref, left, right in ((first_ref, out_a, out_b), (second_ref, out_c, out_d)):
            even, odd = ref[2 * pair], ref[2 * pair + 1]
            left[:, cols] = jnp.concatenate([even[:, :HEAD_DIM], odd[:, :HEAD_DIM]], axis=1)
            right[:, cols] = jnp.concatenate([even[:, HEAD_DIM:], odd[:, HEAD_DIM:]], axis=1)


def ends_of(lengths):
    lines = lengths.shape[0]
    wide = lengths.astype(F32)
    high = wide.astype(BF16)
    low = (wide - high.astype(F32)).astype(BF16)
    row = lax.broadcasted_iota(jnp.int32, (LANES, LANES), 0)
    col = lax.broadcasted_iota(jnp.int32, (LANES, LANES), 1)
    upto = jnp.where(row <= col, 1.0, 0.0).astype(BF16)
    within = dot(high, upto, 1, 0) + dot(low, upto, 1, 0)
    offset = jnp.zeros((1, 1), F32)
    ends = []
    for line in range(lines):
        ends.append(within[line : line + 1] + offset)
        offset = ends[-1][:, LANES - 1 :]
    return ends


def count_ends(ends, positions):
    count = jnp.zeros((positions.shape[0], LANES), F32)
    for line in ends:
        count = count + jnp.where(line <= positions, 1.0, 0.0)
    return jnp.sum(count, axis=1, keepdims=True)


def run_of(slot, owners):
    second = jnp.where(slot >= owners, 1, 0)
    group = slot - second * owners
    odd = lax.rem(group, 2)
    return (group - odd) * 2 + odd + second * 2


def chain_matrices(ends, run_rows, owners):
    slots = 2 * owners
    first_at = (run_of(lax.broadcasted_iota(jnp.int32, (LANES, 1), 0), owners) * run_rows).astype(F32)
    first = jnp.broadcast_to(count_ends(ends, first_at), (LANES, LANES))
    last = jnp.broadcast_to(count_ends(ends, first_at + (run_rows - 1.0)), (LANES, LANES))
    mine = run_of(lax.broadcasted_iota(jnp.int32, (LANES, LANES), 0), owners)
    other = run_of(lax.broadcasted_iota(jnp.int32, (LANES, LANES), 1), owners)
    rising = jnp.where((jnp.transpose(last) == first) & (other < mine), 1.0, 0.0)
    falling = jnp.where((jnp.transpose(first) == last) & (other > mine), 1.0, 0.0)
    return rising[:slots, :slots].astype(BF16), falling[:slots, :slots].astype(BF16)


def lanes_of(rows):
    return lax.broadcasted_iota(jnp.int32, (rows, LANES), 1)


def turn(x, by):
    by = by % LANES
    return pltpu.roll(x, by, 1) if by else x


def store_pieces(ref, sums, totals):
    owners = ref.shape[0]
    share = FEATURES // owners
    line = jnp.zeros((owners, LANES), F32)
    for i in range(share):
        part = slice(i * owners, (i + 1) * owners)
        for run in range(2):
            ref[:, run * share + i, :] = sums[run][part]
        line = line + turn(totals[part], 4 * i)
    ref[:, 2 * share, :] = line


def load_pieces(ref):
    owners = ref.shape[0]
    share = FEATURES // owners
    line = ref[:, 2 * share, :]
    totals = jnp.concatenate([turn(line, -4 * i) for i in range(share)], axis=0)
    totals = jnp.where(lanes_of(FEATURES) < 4, totals, 0.0)
    result = []
    for run in range(2):
        sums = jnp.concatenate([ref[:, run * share + i, :] for i in range(share)], axis=0)
        result.append(split2(beside(sums, totals)))
    return result


def chain(rising, falling, in_ref, out_ref):
    owners = in_ref.shape[0]
    share = FEATURES // owners
    lane = lanes_of(owners)
    second = lax.rem(lane, 4) >= 2
    blocks = []
    for i in range(share):
        blocks.append(jnp.concatenate([in_ref[:, i, :], in_ref[:, share + i, :]], axis=0))
    line = in_ref[:, 2 * share, :]
    blocks.append(
        jnp.concatenate([jnp.where(second, 0.0, line), turn(jnp.where(second, line, 0.0), -2)], axis=0)
    )
    side = lanes_of(2 * owners)
    for i, block in enumerate(blocks):
        parts = split3(block)
        up = dot(rising, parts[0], 1, 0) + dot(rising, parts[1], 1, 0) + dot(rising, parts[2], 1, 0)
        down = dot(falling, parts[0], 1, 0) + dot(falling, parts[1], 1, 0) + dot(falling, parts[2], 1, 0)
        if i < share:
            both = jnp.where(side < HEAD_DIM, up, down)
            out_ref[:, i, :] = both[:owners]
            out_ref[:, share + i, :] = both[owners:]
        else:
            both = jnp.where(lax.rem(side, 2) == 0, up, down)
            out_ref[:, 2 * share, :] = both[:owners] + turn(both[owners:], 2)


def over_peers(size, step):
    group = 7 if (size - 1) % 7 == 0 else 1

    def several(turn, carry):
        for i in range(group):
            step(turn * group + i + 1)
        return carry

    lax.fori_loop(0, (size - 1) // group, several, 0)


class Place:
    def __init__(self):
        self.wide = lax.axis_index("wide")
        self.narrow = lax.axis_index("narrow")
        self.second = lax.rem(self.wide, 2)
        self.quarter = lax.rem(self.narrow, 4)
        self.half = lax.div(self.narrow, 4)
        self.even = self.wide - self.second
        self.member = self.second * 4 + self.quarter
        self.group = self.even + self.half

    def of_member(self, member):
        quarter = lax.rem(member, 4)
        return {"wide": self.even + lax.div(member, 4), "narrow": self.half * 4 + quarter}

    def of_group(self, group):
        half = lax.rem(group, 2)
        return {"wide": group - half + self.second, "narrow": half * 4 + self.quarter}


class Exchange:
    def __init__(self, me, device_of, send, land, send_sem, recv_sem):
        self.me, self.device_of, self.size = me, device_of, send.shape[0]
        self.send, self.land, self.send_sem, self.recv_sem = send, land, send_sem, recv_sem

    def start(self):
        def step(offset):
            peer = lax.rem(self.me + offset, self.size)
            pltpu.make_async_remote_copy(
                src_ref=self.send.at[peer],
                dst_ref=self.land.at[self.me],
                send_sem=self.send_sem,
                recv_sem=self.recv_sem,
                device_id=self.device_of(peer),
                device_id_type=MESH,
            ).start()

        over_peers(self.size, step)
        self.land[self.me] = self.send[self.me]

    def all_but_one(self):
        part = pl.ds(0, self.size - 1)
        return pltpu.make_async_remote_copy(
            src_ref=self.send.at[part],
            dst_ref=self.land.at[part],
            send_sem=self.send_sem,
            recv_sem=self.recv_sem,
            device_id=self.device_of(lax.rem(self.me + 1, self.size)),
            device_id_type=MESH,
        )

    def arrived(self):
        self.all_but_one().wait_recv()

    def sent(self):
        self.all_but_one().wait_send()


def main_kernel(
    q_any, k_any, v_any, g_any, lengths_ref, proj_ref,
    first_ref, second_ref,
    q_ref, k_ref, v_ref, g_ref,
    kv_send, kv_ref, qg_send, qg_ref,
    piece, gathered, moved, state, piece_g, gathered_g, moved_g, state_g,
    done_q, back_q, done_k, back_k,
    phi_k_ref, phi_q_ref, expo_k_ref, expo_q_ref, ids_ref, a_ref, total_ref,
    score_high, score_low, coupling_high, coupling_low, key_up_ref, value_up_ref,
    in_sem, send_sem, recv_sem,
):
    fine = kv_send.shape[0]
    coarse = piece.shape[0]
    own = q_ref.shape[0]
    rows = own * fine
    run_rows = rows // 2
    strips = rows // STRIP
    blocks = STRIP // own
    here = Place()

    def within(number, send, land):
        return Exchange(here.member, here.of_member, send, land, send_sem.at[number], recv_sem.at[number])

    def across(number, send, land):
        return Exchange(here.group, here.of_group, send, land, send_sem.at[number], recv_sem.at[number])

    move_kv = within(0, kv_send, kv_ref)
    move_qg = within(1, qg_send, qg_ref)
    gather_s = across(2, piece, gathered)
    scatter_s = across(3, moved, state)
    gather_g = across(4, piece_g, gathered_g)
    scatter_g = across(5, moved_g, state_g)
    give_q = within(6, done_q, back_q)
    give_k = within(7, done_k, back_k)

    barrier = pltpu.get_barrier_semaphore()

    def greet(me, device_of, size):
        def step(offset):
            pl.semaphore_signal(
                barrier, inc=1, device_id=device_of(lax.rem(me + offset, size)), device_id_type=MESH
            )

        over_peers(size, step)

    greet(here.member, here.of_member, fine)
    greet(here.group, here.of_group, coarse)
    loads = [
        pltpu.make_async_copy(source, target, in_sem.at[i])
        for i, (source, target) in enumerate(
            ((k_any, k_ref), (v_any, v_ref), (q_any, q_ref), (g_any, g_ref))
        )
    ]
    for load in loads:
        load.start()

    def pack(left, right, target):
        for head in range(fine):
            cols = slice(head * HEAD_DIM, (head + 1) * HEAD_DIM)
            target[head] = beside(left[:, cols], right[:, cols])

    loads[0].wait()
    loads[1].wait()
    pack(k_ref, v_ref, kv_send)
    pl.semaphore_wait(barrier, fine - 1 + coarse - 1)
    move_kv.start()
    loads[2].wait()
    loads[3].wait()
    pack(q_ref, g_ref, qg_send)
    move_qg.start()

    projection = proj_ref[...]
    parts = split3(projection * INV_ROOT)
    mix_parts = jnp.concatenate([parts[0], parts[1], parts[2], jnp.zeros_like(parts[0])], axis=0)
    below = lax.broadcasted_iota(jnp.int32, projection.shape, 0) == 0
    grad_parts = split2(jnp.concatenate([projection, jnp.where(below, 1.0, 0.0)], axis=0))

    ends = ends_of(lengths_ref[...])
    rising, falling = chain_matrices(ends, run_rows, coarse)
    first_run = 2 * here.even + here.half

    class Strip:
        def __init__(self, number):
            self.at = slice(number * STRIP, (number + 1) * STRIP)
            self.slots = slice(number * blocks, (number + 1) * blocks)
            self.run = number * STRIP // run_rows
            self.whole = slice(self.run * run_rows, (self.run + 1) * run_rows)
            inside = number * STRIP - self.run * run_rows
            start = ((first_run + 2 * self.run) * run_rows + inside).astype(F32)
            self.places = lax.broadcasted_iota(jnp.int32, (STRIP, 1), 0).astype(F32) + start

        def of(self, ref):
            return ref[self.slots].reshape(STRIP, LANES)

        def sides(self):
            ids = ids_ref[self.at, :]
            ends_at = self.whole
            return ids == ids_ref[ends_at.start : ends_at.start + 1, :], ids == ids_ref[ends_at.stop - 1 : ends_at.stop, :]

        def mask(self):
            return ids_ref[self.at, :1] == id_row[:, self.whole]

        def pair(self, left, left_use, right, right_use):
            return beside(
                jnp.where(left_use[:, :HEAD_DIM], left, 0.0), jnp.where(right_use[:, :HEAD_DIM], right, 0.0)
            )

        def line(self, left_use, right_use, amount):
            lane = lanes_of(STRIP) - 2 * self.run
            use = ((lane == 0) & left_use) | ((lane == 1) & right_use)
            return jnp.where(use, jnp.broadcast_to(amount, (STRIP, LANES)), 0.0)

    every = [Strip(number) for number in range(strips)]
    for strip in every:
        ids_ref[strip.at, :] = jnp.broadcast_to(count_ends(ends, strip.places), (STRIP, LANES))
    id_row = jnp.transpose(ids_ref[...])[:1, :]
    ones = jnp.ones((STRIP, 1), F32)

    def pieces_of(phi_ref, weights):
        sums, totals = [], jnp.zeros((FEATURES, LANES), F32)
        for run in range(2):
            found = 0.0
            for strip, weight in zip(every, weights):
                if strip.run == run:
                    for part in weight:
                        found = found + dot(phi_ref[strip.at, :], part, 0, 0)
            sums.append(found[:, :LANES])
            totals = totals + found[:, LANES:]
        return sums, totals

    move_kv.arrived()
    weights = []
    for strip in every:
        packed = strip.of(kv_ref)
        expo, phi = features(packed[:, :HEAD_DIM], mix_parts)
        expo_k_ref[strip.at, :] = expo
        phi_k_ref[strip.at, :] = phi
        front, back = strip.sides()
        vectors = packed[:, HEAD_DIM:].astype(F32)
        weights.append([beside(strip.pair(vectors, back, vectors, front), strip.line(back, front, ones)).astype(BF16)])
    store_pieces(piece, *pieces_of(phi_k_ref, weights))
    gather_s.start()

    def values_of(run):
        packed = kv_ref[run * fine // 2 : (run + 1) * fine // 2].reshape(run_rows, LANES)
        return extended(packed[:, HEAD_DIM:].astype(F32), jnp.ones((run_rows, 1), F32)).astype(BF16)

    values = [values_of(run) for run in range(2)]

    move_qg.arrived()
    for strip in every:
        expo, phi = features(strip.of(qg_ref)[:, :HEAD_DIM], mix_parts)
        expo_q_ref[strip.at, :] = expo
        phi_q_ref[strip.at, :] = phi
        scores = jnp.where(strip.mask(), dot(phi, phi_k_ref[strip.whole, :], 1, 1), 0.0)
        score_high[strip.at, :], score_low[strip.at, :] = split2(scores)

    gather_s.arrived()
    chain(rising, falling, gathered, moved)
    scatter_s.start()

    for strip in every:
        total_ref[strip.at, :] = dot(score_high[strip.at, :], values[strip.run], 1, 0) + dot(
            score_low[strip.at, :], values[strip.run], 1, 0
        )

    scatter_s.arrived()
    states = load_pieces(state)
    weights = []
    for strip in every:
        front, back = strip.sides()
        phi = phi_q_ref[strip.at, :]
        grad = strip.of(qg_ref)[:, HEAD_DIM:].astype(F32)
        high, low = states[strip.run]
        far = dot(phi, high, 1, 0) + dot(phi, low, 1, 0)
        total = total_ref[strip.at, :]
        numer = total[:, :HEAD_DIM]
        numer = numer + jnp.where(front[:, :HEAD_DIM], far[:, :HEAD_DIM], 0.0)
        numer = numer + jnp.where(back[:, :HEAD_DIM], far[:, HEAD_DIM:LANES], 0.0)
        lane = LANES + 2 * strip.run
        denom = total[:, HEAD_DIM : HEAD_DIM + 1]
        denom = denom + jnp.where(front[:, :1], far[:, lane : lane + 1], 0.0)
        denom = denom + jnp.where(back[:, :1], far[:, lane + 1 : lane + 2], 0.0)
        inverse = 1.0 / denom
        attended = numer * inverse
        total_ref[strip.at, :HEAD_DIM] = attended
        bias = -jnp.sum(grad * attended, axis=1, keepdims=True) * inverse
        a = grad * inverse
        a_ref[strip.at, :] = extended(a, bias)
        weights.append(split2(beside(strip.pair(a, back, a, front), strip.line(back, front, bias))))
    store_pieces(piece_g, *pieces_of(phi_q_ref, weights))
    gather_g.start()

    for strip in every:
        front, back = strip.sides()
        a = a_ref[strip.at, :]
        bias = a[:, HEAD_DIM : HEAD_DIM + 1]
        doubled = beside(values[strip.run], values[strip.run])
        coupling = jnp.where(strip.mask(), dot(beside(*split2(a)), doubled, 1, 1), 0.0)
        high, low = split2(coupling)
        coupling_high[strip.at, :] = high
        coupling_low[strip.at, :] = low
        phi_k = phi_k_ref[strip.whole, :]
        up = dot(high, phi_k, 1, 0) + dot(low, phi_k, 1, 0)
        vectors = a[:, :HEAD_DIM]
        use_high, use_low = split2(beside(strip.pair(vectors, front, vectors, back), strip.line(front, back, bias)))
        high, low = states[strip.run]
        up = up + dot(use_high, high, 1, 1) + dot(use_high, low, 1, 1) + dot(use_low, high, 1, 1)
        query_grad = feature_grad(strip.of(qg_ref)[:, :HEAD_DIM], expo_q_ref[strip.at, :], up, grad_parts)
        done = beside(total_ref[strip.at, :HEAD_DIM], query_grad).astype(BF16)
        done_q[strip.slots] = done.reshape(blocks, own, LANES)
    give_q.start()

    gather_g.arrived()
    chain(rising, falling, gathered_g, moved_g)
    scatter_g.start()

    for run in range(2):
        whole = slice(run * run_rows, (run + 1) * run_rows)
        a_high, a_low = split2(a_ref[whole, :])
        high = score_high[whole, :]
        both = dot(beside(a_high, a_low), high, 0, 0)
        value_up_ref[:, whole] = both[:LANES] + both[LANES:] + dot(a_high, score_low[whole, :], 0, 0)
        phi = phi_q_ref[whole, :]
        key_up_ref[:, whole] = dot(phi, coupling_high[whole, :], 0, 0) + dot(phi, coupling_low[whole, :], 0, 0)

    scatter_g.arrived()
    states = load_pieces(state_g)
    for strip in every:
        front, back = strip.sides()
        phi = phi_k_ref[strip.at, :]
        packed = strip.of(kv_ref)
        vectors = packed[:, HEAD_DIM:].astype(F32)
        use = beside(strip.pair(vectors, front, vectors, back), strip.line(front, back, ones)).astype(BF16)
        high, low = states[strip.run]
        up = jnp.transpose(key_up_ref[:, strip.at]) + dot(use, high, 1, 1) + dot(use, low, 1, 1)
        far = dot(phi, high[:, :LANES], 1, 0) + dot(phi, low[:, :LANES], 1, 0)
        total = jnp.transpose(value_up_ref[:, strip.at])[:, :HEAD_DIM]
        total = total + jnp.where(front[:, :HEAD_DIM], far[:, :HEAD_DIM], 0.0)
        total = total + jnp.where(back[:, :HEAD_DIM], far[:, HEAD_DIM:], 0.0)
        key_grad = feature_grad(packed[:, :HEAD_DIM], expo_k_ref[strip.at, :], up, grad_parts)
        done_k[strip.slots] = beside(key_grad, total).astype(BF16).reshape(blocks, own, LANES)
    give_k.start()

    give_q.arrived()
    first_ref[...] = back_q[...]
    give_k.arrived()
    second_ref[...] = back_k[...]
    for each in (move_kv, move_qg, gather_s, scatter_s, gather_g, scatter_g, give_q, give_k):
        each.sent()


def body(coarse, fine, query_rows, key_rows, value_rows, out_grad, doc_lengths, projection):
    own = query_rows.shape[0]
    rows = own * fine
    shape = jax.ShapeDtypeStruct
    packed = shape((fine, own, LANES), BF16)
    lines = 2 * FEATURES // coarse + 1
    vmem = pl.BlockSpec(memory_space=pltpu.VMEM)
    anywhere = pl.BlockSpec(memory_space=pl.ANY)
    tokens = pltpu.VMEM(query_rows.shape, BF16)
    blocks = pltpu.VMEM((fine, own, LANES), BF16)
    pieces = pltpu.VMEM((coarse, lines, LANES), F32)
    narrow_rows = pltpu.VMEM((rows, LANES), BF16)
    wide_rows = pltpu.VMEM((rows, LANES), F32)
    square = pltpu.VMEM((rows, rows // 2), BF16)
    turned = pltpu.VMEM((LANES, rows), F32)
    scratch = [tokens] * 4 + [blocks] * 4 + [pieces] * 8 + [blocks] * 4
    scratch += [narrow_rows] * 2 + [wide_rows] * 5 + [square] * 4 + [turned] * 2
    scratch += [pltpu.SemaphoreType.DMA((count,)) for count in (4, 8, 8)]
    first, second = pl.pallas_call(
        main_kernel,
        out_shape=(packed, packed),
        in_specs=[anywhere] * 4 + [vmem] * 2,
        out_specs=(vmem, vmem),
        scratch_shapes=scratch,
        compiler_params=pltpu.CompilerParams(
            collective_id=0, has_side_effects=True, vmem_limit_bytes=VMEM_BYTES
        ),
        cost_estimate=pl.CostEstimate(
            flops=2 * rows * rows * LANES * 6, bytes_accessed=8 * own * fine * HEAD_DIM * 2, transcendentals=0
        ),
    )(query_rows, key_rows, value_rows, out_grad, doc_lengths.reshape(-1, LANES), projection.T)
    out = shape(query_rows.shape, BF16)
    return pl.pallas_call(
        unpack_kernel,
        out_shape=(out, out, out, out),
        in_specs=[vmem] * 2,
        out_specs=(vmem,) * 4,
        compiler_params=pltpu.CompilerParams(vmem_limit_bytes=VMEM_BYTES),
        cost_estimate=pl.CostEstimate(flops=0, bytes_accessed=8 * own * fine * HEAD_DIM * 2, transcendentals=0),
    )(first, second)


def solution(mesh):
    tokens = P(("wide", "narrow"), None)
    return jax.shard_map(
        functools.partial(body, mesh.shape["wide"], mesh.shape["narrow"]),
        mesh=mesh,
        in_specs=(tokens, tokens, tokens, tokens, P(), P()),
        out_specs=(tokens, tokens, tokens, tokens),
        check_vma=False,
    )
```

time: 162 us -> 77.5 us (0.48)
  blocking collectives: 92 us -> 0 us
  Pallas kernels: 17 us -> 76.7 us
  starting transfers between devices: 24.2 us -> 0 us
  waiting for transfers between devices: 23.1 us -> 0 us
  local copies, waits for them, and re-layouts: 4.26 us -> 0 us
    all_to_all x5 -> x0, blocking collectives: 92 us -> none  [exchange(): return lax.all_to_all(x, axis, split_axis=0, concat_axis=0, tiled=True)]
    pallas_call x7 -> x2, Pallas kernels: 17 us -> 76.7 us  [the longest x1 74.7 us: body(): pl.pallas_call(main_kernel, out_shape=(packed, packed), in_specs=[anywher...]
    all_to_all x3 -> x0, starting transfers between devices: 24.2 us -> none  [exchange(): return lax.all_to_all(x, axis, split_axis=0, concat_axis=0, tiled=True)]
    all_to_all x3 -> x0, waiting for transfers between devices: 23.1 us -> none  [exchange(): return lax.all_to_all(x, axis, split_axis=0, concat_axis=0, tiled=True)]
    unnamed x13 -> x0, local copies, waits for them, and re-layouts: 4.07 us -> none
  transfers between devices with their start and end apart: 3 -> 0, of which waited for: 3 -> 0; matrix products, arithmetic and copies ran while one was open for 0% -> 0% of each run, Pallas kernels for 1% -> 0%
where the time goes in v2:
time: 77.5 us; the launch traced here: 77.3 us
  Pallas kernels  76.7 us (99%)
    pallas_call x1, Pallas kernels, body(): pl.pallas_call(main_kernel, out_shape=(packed, packed), in_specs=[anywher...  74.7 us
    pallas_call x1, Pallas kernels, body(): pl.pallas_call(unpack_kernel, out_shape=(out, out, out, out), in_specs=[v...  1.99 us

profile of v2, /device:TPU:1, one launch (start us, length us, event | category | flops | bytes accessed | tf_op | source)
XLA Modules:
  0.0 77.3 jit_solution(4593616490562657296)
XLA Ops:
  0.6 74.7 %shard_map.93 = (bf16[8,128,128]{2,1,0:T(8,128)(2,1)}, bf16[8,128,128]{2,1,0:T(8,128)(2,1)}) custom-call(bf16[128,512]{1,0:T(8,128)(2,1)} %q_any.1, bf16[128,512]{1,0:T(8,128)(2,1)} %k_any.1, bf16[128,512]{1,0:T(8,128)(2,1)} %v_any.1, bf16[128,512]{1,0:T(8,128)(2,1)} %g_any.1, s32[8,128]{1,0:T(8,128)} %bitcast.3, f32[64,128]{1,0:T(8,128)} %bitcast.2), custom_call_target="tpu_custom_call" | custom-call | flops 1610612736 | bytes 1048576 | tf_op jit(solution)/shard_map/pallas_call | solution.py:516
  75.3 2.0 %shard_map.94 = (bf16[128,512]{1,0:T(8,128)(2,1)}, bf16[128,512]{1,0:T(8,128)(2,1)}, bf16[128,512]{1,0:T(8,128)(2,1)}, bf16[128,512]{1,0:T(8,128)(2,1)}) custom-call(bf16[8,128,128]{2,1,0:T(8,128)(2,1)} %get-tuple-element.6.first_ref, bf16[8,128,128]{2,1,0:T(8,128)(2,1)} %get-tuple-element.7.second_ref), custom_call_target="tpu_custom_call" | custom-call | bytes 1048576 | tf_op jit(solution)/shard_map/pallas_call | solution.py:530

commit v3 on v2

--- a/solution.py
+++ b/solution.py
@@ -18,6 +18,7 @@
 VMEM_BYTES = 56 * 1024 * 1024
 MESH = pl.DeviceIdType.MESH
 STRIP = 256
+LINE = 8
 
 
 def dot(a, b, da, db):
@@ -95,83 +96,118 @@
     return jnp.sum(count, axis=1, keepdims=True)
 
 
-def run_of(slot, owners):
-    second = jnp.where(slot >= owners, 1, 0)
-    group = slot - second * owners
-    odd = lax.rem(group, 2)
-    return (group - odd) * 2 + odd + second * 2
-
-
-def chain_matrices(ends, run_rows, owners):
-    slots = 2 * owners
-    first_at = (run_of(lax.broadcasted_iota(jnp.int32, (LANES, 1), 0), owners) * run_rows).astype(F32)
-    first = jnp.broadcast_to(count_ends(ends, first_at), (LANES, LANES))
-    last = jnp.broadcast_to(count_ends(ends, first_at + (run_rows - 1.0)), (LANES, LANES))
-    mine = run_of(lax.broadcasted_iota(jnp.int32, (LANES, LANES), 0), owners)
-    other = run_of(lax.broadcasted_iota(jnp.int32, (LANES, LANES), 1), owners)
-    rising = jnp.where((jnp.transpose(last) == first) & (other < mine), 1.0, 0.0)
-    falling = jnp.where((jnp.transpose(first) == last) & (other > mine), 1.0, 0.0)
-    return rising[:slots, :slots].astype(BF16), falling[:slots, :slots].astype(BF16)
-
-
 def lanes_of(rows):
     return lax.broadcasted_iota(jnp.int32, (rows, LANES), 1)
 
 
-def turn(x, by):
-    by = by % LANES
-    return pltpu.roll(x, by, 1) if by else x
+def totals_in_rows(totals):
+    return jnp.transpose(totals)[:8]
 
 
 def store_pieces(ref, sums, totals):
     owners = ref.shape[0]
     share = FEATURES // owners
-    line = jnp.zeros((owners, LANES), F32)
-    for i in range(share):
-        part = slice(i * owners, (i + 1) * owners)
+    for run in range(2):
+        ref[:, run * share : (run + 1) * share, :] = sums[run].reshape(owners, share, LANES)
+    ref[:, 2 * share :, :] = jnp.broadcast_to(totals_in_rows(totals)[None], (owners, 8, LANES))
+
+
+class Chain:
+    def __init__(self, ends, here, run_rows, inner, outer, row_coef, line_coef, own_coef, ids_of):
+        self.inner, self.outer, self.share = inner, outer, FEATURES // inner
+        self.row_coef, self.line_coef, self.own_coef = row_coef, line_coef, own_coef
+        runs = 2 * inner
+        size = runs + outer
+        slot = lax.broadcasted_iota(jnp.int32, (size, 1), 0)
+        odd = jnp.where(lax.rem(slot, 4) >= 2, 1, 0)
+        of_run = here.line * runs + slot + lax.rem(slot, 2) - odd
+        index = jnp.where(slot < runs, of_run, (slot - runs) * runs)
+        start = (index * run_rows).astype(F32)
+        length = jnp.where(slot < runs, run_rows, run_rows * runs).astype(F32)
+        first = jnp.broadcast_to(count_ends(ends, start), (size, LANES))
+        last = jnp.broadcast_to(count_ends(ends, start + length - 1.0), (size, LANES))
+        start = jnp.broadcast_to(start, (size, LANES))
+        valid = jnp.broadcast_to(slot - runs, (size, LANES)) != here.line
+        left = lanes_of(size) < HEAD_DIM
+
+        def relation(start_r, first_r, last_r):
+            rising = valid & (last == first_r) & (start < start_r)
+            falling = valid & (first == last_r) & (start > start_r)
+            return jnp.where(rising, 1.0, 0.0), jnp.where(falling, 1.0, 0.0)
+
+        for run in range(runs):
+            at = slice(run, run + 1)
+            rising, falling = relation(start[at], first[at], last[at])
+            row_coef[run] = jnp.where(left, rising, falling)
         for run in range(2):
-            ref[:, run * share + i, :] = sums[run][part]
-        line = line + turn(totals[part], 4 * i)
-    ref[:, 2 * share, :] = line
-
-
-def load_pieces(ref):
-    owners = ref.shape[0]
-    share = FEATURES // owners
-    line = ref[:, 2 * share, :]
-    totals = jnp.concatenate([turn(line, -4 * i) for i in range(share)], axis=0)
-    totals = jnp.where(lanes_of(FEATURES) < 4, totals, 0.0)
-    result = []
-    for run in range(2):
-        sums = jnp.concatenate([ref[:, run * share + i, :] for i in range(share)], axis=0)
-        result.append(split2(beside(sums, totals)))
-    return result
-
-
-def chain(rising, falling, in_ref, out_ref):
-    owners = in_ref.shape[0]
-    share = FEATURES // owners
-    lane = lanes_of(owners)
-    second = lax.rem(lane, 4) >= 2
-    blocks = []
-    for i in range(share):
-        blocks.append(jnp.concatenate([in_ref[:, i, :], in_ref[:, share + i, :]], axis=0))
-    line = in_ref[:, 2 * share, :]
-    blocks.append(
-        jnp.concatenate([jnp.where(second, 0.0, line), turn(jnp.where(second, line, 0.0), -2)], axis=0)
-    )
-    side = lanes_of(2 * owners)
-    for i, block in enumerate(blocks):
-        parts = split3(block)
-        up = dot(rising, parts[0], 1, 0) + dot(rising, parts[1], 1, 0) + dot(rising, parts[2], 1, 0)
-        down = dot(falling, parts[0], 1, 0) + dot(falling, parts[1], 1, 0) + dot(falling, parts[2], 1, 0)
-        if i < share:
-            both = jnp.where(side < HEAD_DIM, up, down)
-            out_ref[:, i, :] = both[:owners]
-            out_ref[:, share + i, :] = both[owners:]
-        else:
-            both = jnp.where(lax.rem(side, 2) == 0, up, down)
-            out_ref[:, 2 * share, :] = both[:owners] + turn(both[owners:], 2)
+            begin = ((here.first_run + 2 * run) * run_rows).astype(F32)
+            own_coef[2 * run], own_coef[2 * run + 1] = relation(begin, *ids_of(run))
+        line_coef[0] = jnp.where(last == last[runs - 1 : runs], 1.0, 0.0)
+        line_coef[1] = jnp.where(first == first[:1], 1.0, 0.0)
+        line_coef[2] = jnp.where(left, line_coef[0], line_coef[1])
+
+    def block(self, gathered, run):
+        return gathered[run // 2, (run % 2) * self.share : (run % 2 + 1) * self.share, :]
+
+    def total(self, gathered, run, side):
+        row = 2 * self.share + 2 * (run % 2) + side
+        return gathered[run // 2, row : row + 1, :]
+
+    def sum_line(self, gathered, out):
+        found = jnp.zeros((self.share, LANES), F32)
+        totals = [jnp.zeros((1, LANES), F32)] * 2
+        for run in range(2 * self.inner):
+            found = found + self.line_coef[2, run : run + 1, :] * self.block(gathered, run)
+            for side in range(2):
+                totals[side] = totals[side] + self.line_coef[side, run : run + 1, :] * self.total(gathered, run, side)
+        out[: self.share, :] = found
+        out[self.share :, :] = jnp.concatenate(totals + [jnp.zeros((6, LANES), F32)], axis=0)
+
+    def place(self, run):
+        return run // 2, slice((run % 2) * self.share, (run % 2 + 1) * self.share)
+
+    def from_line(self, gathered, out):
+        runs = 2 * self.inner
+        blocks = [self.block(gathered, run) for run in range(runs)]
+        for run in range(runs):
+            found = jnp.zeros((self.share, LANES), F32)
+            for source in range(runs):
+                if source != run:
+                    found = found + self.row_coef[run, source : source + 1, :] * blocks[source]
+            owner, at = self.place(run)
+            out[owner, at, :] = found
+
+    def from_lines(self, lines, out):
+        runs = 2 * self.inner
+        blocks = [lines[line, : self.share, :] for line in range(self.outer)]
+        for run in range(runs):
+            owner, at = self.place(run)
+            found = out[owner, at, :]
+            for line in range(self.outer):
+                source = runs + line
+                found = found + self.row_coef[run, source : source + 1, :] * blocks[line]
+            out[owner, at, :] = found
+
+    def totals(self, gathered, lines):
+        runs = 2 * self.inner
+        rows = []
+        for row in range(4):
+            side = row % 2
+            found = jnp.zeros((1, LANES), F32)
+            for source in range(runs):
+                found = found + self.own_coef[row, source : source + 1, :] * self.total(gathered, source, side)
+            for line in range(self.outer):
+                at = self.share + side
+                found = found + self.own_coef[row, runs + line : runs + line + 1, :] * lines[line, at : at + 1, :]
+            rows.append(found)
+        return jnp.transpose(jnp.concatenate(rows + [jnp.zeros((LANES - 4, LANES), F32)], axis=0))
+
+    def states(self, state, totals):
+        result = []
+        for run in range(2):
+            sums = state[:, run * self.share : (run + 1) * self.share, :].reshape(FEATURES, LANES)
+            result.append(split2(beside(sums, totals)))
+        return result
 
 
 def over_peers(size, step):
@@ -194,27 +230,33 @@
         self.half = lax.div(self.narrow, 4)
         self.even = self.wide - self.second
         self.member = self.second * 4 + self.quarter
-        self.group = self.even + self.half
+        self.line = lax.div(self.wide, LINE)
+        self.base = self.line * LINE
+        self.inside = self.even - self.base + self.half
+        self.first_run = 2 * self.even + self.half
 
     def of_member(self, member):
         quarter = lax.rem(member, 4)
         return {"wide": self.even + lax.div(member, 4), "narrow": self.half * 4 + quarter}
 
-    def of_group(self, group):
-        half = lax.rem(group, 2)
-        return {"wide": group - half + self.second, "narrow": half * 4 + self.quarter}
+    def of_inside(self, inside):
+        half = lax.rem(inside, 2)
+        return {"wide": self.base + inside - half + self.second, "narrow": half * 4 + self.quarter}
+
+    def of_line(self, line):
+        return {"wide": self.wide - self.base + line * LINE, "narrow": self.narrow}
 
 
 class Exchange:
-    def __init__(self, me, device_of, send, land, send_sem, recv_sem):
-        self.me, self.device_of, self.size = me, device_of, send.shape[0]
+    def __init__(self, me, device_of, send, land, send_sem, recv_sem, same=False):
+        self.me, self.device_of, self.size, self.same = me, device_of, land.shape[0], same
         self.send, self.land, self.send_sem, self.recv_sem = send, land, send_sem, recv_sem
 
     def start(self):
         def step(offset):
             peer = lax.rem(self.me + offset, self.size)
             pltpu.make_async_remote_copy(
-                src_ref=self.send.at[peer],
+                src_ref=self.send if self.same else self.send.at[peer],
                 dst_ref=self.land.at[self.me],
                 send_sem=self.send_sem,
                 recv_sem=self.recv_sem,
@@ -223,13 +265,13 @@
             ).start()
 
         over_peers(self.size, step)
-        self.land[self.me] = self.send[self.me]
+        self.land[self.me] = self.send[...] if self.same else self.send[self.me]
 
     def all_but_one(self):
-        part = pl.ds(0, self.size - 1)
+        part = self.land.at[pl.ds(0, self.size - 1)]
         return pltpu.make_async_remote_copy(
-            src_ref=self.send.at[part],
-            dst_ref=self.land.at[part],
+            src_ref=part,
+            dst_ref=part,
             send_sem=self.send_sem,
             recv_sem=self.recv_sem,
             device_id=self.device_of(lax.rem(self.me + 1, self.size)),
@@ -248,14 +290,15 @@
     first_ref, second_ref,
     q_ref, k_ref, v_ref, g_ref,
     kv_send, kv_ref, qg_send, qg_ref,
-    piece, gathered, moved, state, piece_g, gathered_g, moved_g, state_g,
+    piece, gathered, line, lines, moved, state, piece_g, gathered_g, line_g, lines_g, moved_g, state_g,
+    row_coef, line_coef, own_coef,
     done_q, back_q, done_k, back_k,
     phi_k_ref, phi_q_ref, expo_k_ref, expo_q_ref, ids_ref, a_ref, total_ref,
     score_high, score_low, coupling_high, coupling_low, key_up_ref, value_up_ref,
     in_sem, send_sem, recv_sem,
 ):
     fine = kv_send.shape[0]
-    coarse = piece.shape[0]
+    inner, outer = piece.shape[0], lines.shape[0]
     own = q_ref.shape[0]
     rows = own * fine
     run_rows = rows // 2
@@ -267,16 +310,21 @@
         return Exchange(here.member, here.of_member, send, land, send_sem.at[number], recv_sem.at[number])
 
     def across(number, send, land):
-        return Exchange(here.group, here.of_group, send, land, send_sem.at[number], recv_sem.at[number])
+        return Exchange(here.inside, here.of_inside, send, land, send_sem.at[number], recv_sem.at[number])
+
+    def lengthwise(number, send, land):
+        return Exchange(here.line, here.of_line, send, land, send_sem.at[number], recv_sem.at[number], True)
 
     move_kv = within(0, kv_send, kv_ref)
     move_qg = within(1, qg_send, qg_ref)
     gather_s = across(2, piece, gathered)
-    scatter_s = across(3, moved, state)
-    gather_g = across(4, piece_g, gathered_g)
-    scatter_g = across(5, moved_g, state_g)
-    give_q = within(6, done_q, back_q)
-    give_k = within(7, done_k, back_k)
+    share_s = lengthwise(3, line, lines)
+    scatter_s = across(4, moved, state)
+    gather_g = across(5, piece_g, gathered_g)
+    share_g = lengthwise(6, line_g, lines_g)
+    scatter_g = across(7, moved_g, state_g)
+    give_q = within(8, done_q, back_q)
+    give_k = within(9, done_k, back_k)
 
     barrier = pltpu.get_barrier_semaphore()
 
@@ -289,7 +337,8 @@
         over_peers(size, step)
 
     greet(here.member, here.of_member, fine)
-    greet(here.group, here.of_group, coarse)
+    greet(here.inside, here.of_inside, inner)
+    greet(here.line, here.of_line, outer)
     loads = [
         pltpu.make_async_copy(source, target, in_sem.at[i])
         for i, (source, target) in enumerate(
@@ -307,7 +356,7 @@
     loads[0].wait()
     loads[1].wait()
     pack(k_ref, v_ref, kv_send)
-    pl.semaphore_wait(barrier, fine - 1 + coarse - 1)
+    pl.semaphore_wait(barrier, fine + inner + outer - 3)
     move_kv.start()
     loads[2].wait()
     loads[3].wait()
@@ -321,8 +370,6 @@
     grad_parts = split2(jnp.concatenate([projection, jnp.where(below, 1.0, 0.0)], axis=0))
 
     ends = ends_of(lengths_ref[...])
-    rising, falling = chain_matrices(ends, run_rows, coarse)
-    first_run = 2 * here.even + here.half
 
     class Strip:
         def __init__(self, number):
@@ -331,7 +378,7 @@
             self.run = number * STRIP // run_rows
             self.whole = slice(self.run * run_rows, (self.run + 1) * run_rows)
             inside = number * STRIP - self.run * run_rows
-            start = ((first_run + 2 * self.run) * run_rows + inside).astype(F32)
+            start = ((here.first_run + 2 * self.run) * run_rows + inside).astype(F32)
             self.places = lax.broadcasted_iota(jnp.int32, (STRIP, 1), 0).astype(F32) + start
 
         def of(self, ref):
@@ -360,6 +407,12 @@
         ids_ref[strip.at, :] = jnp.broadcast_to(count_ends(ends, strip.places), (STRIP, LANES))
     id_row = jnp.transpose(ids_ref[...])[:1, :]
     ones = jnp.ones((STRIP, 1), F32)
+
+    def ids_of(run):
+        begin, end = run * run_rows, (run + 1) * run_rows
+        return ids_ref[begin : begin + 1, :], ids_ref[end - 1 : end, :]
+
+    chain = Chain(ends, here, run_rows, inner, outer, row_coef, line_coef, own_coef, ids_of)
 
     def pieces_of(phi_ref, weights):
         sums, totals = [], jnp.zeros((FEATURES, LANES), F32)
@@ -401,8 +454,13 @@
         score_high[strip.at, :], score_low[strip.at, :] = split2(scores)
 
     gather_s.arrived()
-    chain(rising, falling, gathered, moved)
+    chain.sum_line(gathered, line)
+    share_s.start()
+    chain.from_line(gathered, moved)
+    share_s.arrived()
+    chain.from_lines(lines, moved)
     scatter_s.start()
+    totals = chain.totals(gathered, lines)
 
     for strip in every:
         total_ref[strip.at, :] = dot(score_high[strip.at, :], values[strip.run], 1, 0) + dot(
@@ -410,7 +468,7 @@
         )
 
     scatter_s.arrived()
-    states = load_pieces(state)
+    states = chain.states(state, totals)
     weights = []
     for strip in every:
         front, back = strip.sides()
@@ -436,7 +494,7 @@
     store_pieces(piece_g, *pieces_of(phi_q_ref, weights))
     gather_g.start()
 
-    for strip in every:
+    def query_part(strip):
         front, back = strip.sides()
         a = a_ref[strip.at, :]
         bias = a[:, HEAD_DIM : HEAD_DIM + 1]
@@ -454,11 +512,20 @@
         query_grad = feature_grad(strip.of(qg_ref)[:, :HEAD_DIM], expo_q_ref[strip.at, :], up, grad_parts)
         done = beside(total_ref[strip.at, :HEAD_DIM], query_grad).astype(BF16)
         done_q[strip.slots] = done.reshape(blocks, own, LANES)
+    for strip in every[: strips // 2]:
+        query_part(strip)
+
+    gather_g.arrived()
+    chain.sum_line(gathered_g, line_g)
+    share_g.start()
+    chain.from_line(gathered_g, moved_g)
+    for strip in every[strips // 2 :]:
+        query_part(strip)
+    share_g.arrived()
+    chain.from_lines(lines_g, moved_g)
+    scatter_g.start()
     give_q.start()
-
-    gather_g.arrived()
-    chain(rising, falling, gathered_g, moved_g)
-    scatter_g.start()
+    totals = chain.totals(gathered_g, lines_g)
 
     for run in range(2):
         whole = slice(run * run_rows, (run + 1) * run_rows)
@@ -470,14 +537,14 @@
         key_up_ref[:, whole] = dot(phi, coupling_high[whole, :], 0, 0) + dot(phi, coupling_low[whole, :], 0, 0)
 
     scatter_g.arrived()
-    states = load_pieces(state_g)
+    states_g = chain.states(state_g, totals)
     for strip in every:
         front, back = strip.sides()
         phi = phi_k_ref[strip.at, :]
         packed = strip.of(kv_ref)
         vectors = packed[:, HEAD_DIM:].astype(F32)
         use = beside(strip.pair(vectors, front, vectors, back), strip.line(front, back, ones)).astype(BF16)
-        high, low = states[strip.run]
+        high, low = states_g[strip.run]
         up = jnp.transpose(key_up_ref[:, strip.at]) + dot(use, high, 1, 1) + dot(use, low, 1, 1)
         far = dot(phi, high[:, :LANES], 1, 0) + dot(phi, low[:, :LANES], 1, 0)
         total = jnp.transpose(value_up_ref[:, strip.at])[:, :HEAD_DIM]
@@ -491,7 +558,9 @@
     first_ref[...] = back_q[...]
     give_k.arrived()
     second_ref[...] = back_k[...]
-    for each in (move_kv, move_qg, gather_s, scatter_s, gather_g, scatter_g, give_q, give_k):
+    for each in (
+        move_kv, move_qg, gather_s, share_s, scatter_s, gather_g, share_g, scatter_g, give_q, give_k
+    ):
         each.sent()
 
 
@@ -500,19 +569,26 @@
     rows = own * fine
     shape = jax.ShapeDtypeStruct
     packed = shape((fine, own, LANES), BF16)
-    lines = 2 * FEATURES // coarse + 1
+    share = FEATURES // LINE
+    outer = coarse // LINE
+    sources = 2 * LINE + outer
     vmem = pl.BlockSpec(memory_space=pltpu.VMEM)
     anywhere = pl.BlockSpec(memory_space=pl.ANY)
     tokens = pltpu.VMEM(query_rows.shape, BF16)
     blocks = pltpu.VMEM((fine, own, LANES), BF16)
-    pieces = pltpu.VMEM((coarse, lines, LANES), F32)
+    pieces = pltpu.VMEM((LINE, 2 * share + 8, LANES), F32)
+    results = pltpu.VMEM((LINE, 2 * share, LANES), F32)
+    line_rows = share + 8
+    lines = [pltpu.VMEM((line_rows, LANES), F32), pltpu.VMEM((outer, line_rows, LANES), F32)]
+    phase = [pieces] * 2 + lines + [results] * 2
+    coefs = [pltpu.VMEM((count, sources, LANES), F32) for count in (2 * LINE, 3, 4)]
     narrow_rows = pltpu.VMEM((rows, LANES), BF16)
     wide_rows = pltpu.VMEM((rows, LANES), F32)
     square = pltpu.VMEM((rows, rows // 2), BF16)
     turned = pltpu.VMEM((LANES, rows), F32)
-    scratch = [tokens] * 4 + [blocks] * 4 + [pieces] * 8 + [blocks] * 4
+    scratch = [tokens] * 4 + [blocks] * 4 + phase * 2 + coefs + [blocks] * 4
     scratch += [narrow_rows] * 2 + [wide_rows] * 5 + [square] * 4 + [turned] * 2
-    scratch += [pltpu.SemaphoreType.DMA((count,)) for count in (4, 8, 8)]
+    scratch += [pltpu.SemaphoreType.DMA((count,)) for count in (4, 10, 10)]
     first, second = pl.pallas_call(
         main_kernel,
         out_shape=(packed, packed),

time: 77.5 us -> 77.4 us (level)
  no operation moved by 1% of the time
where the time goes in v3:
time: 77.4 us; the launch traced here: 77.2 us
  Pallas kernels  76.5 us (99%)
    pallas_call x1, Pallas kernels, body(): pl.pallas_call(main_kernel, out_shape=(packed, packed), in_specs=[anywher...  74.6 us
    pallas_call x1, Pallas kernels, body(): pl.pallas_call(unpack_kernel, out_shape=(out, out, out, out), in_specs=[v...  1.99 us

profile of v3, /device:TPU:1, one launch (start us, length us, event | category | flops | bytes accessed | tf_op | source)
XLA Modules:
  0.0 77.2 jit_solution(12675786963995457798)
XLA Ops:
  0.6 74.6 %shard_map.93 = (bf16[8,128,128]{2,1,0:T(8,128)(2,1)}, bf16[8,128,128]{2,1,0:T(8,128)(2,1)}) custom-call(bf16[128,512]{1,0:T(8,128)(2,1)} %q_any.1, bf16[128,512]{1,0:T(8,128)(2,1)} %k_any.1, bf16[128,512]{1,0:T(8,128)(2,1)} %v_any.1, bf16[128,512]{1,0:T(8,128)(2,1)} %g_any.1, s32[8,128]{1,0:T(8,128)} %bitcast.3, f32[64,128]{1,0:T(8,128)} %bitcast.2), custom_call_target="tpu_custom_call" | custom-call | flops 1610612736 | bytes 1048576 | tf_op jit(solution)/shard_map/pallas_call | solution.py:592
  75.2 2.0 %shard_map.94 = (bf16[128,512]{1,0:T(8,128)(2,1)}, bf16[128,512]{1,0:T(8,128)(2,1)}, bf16[128,512]{1,0:T(8,128)(2,1)}, bf16[128,512]{1,0:T(8,128)(2,1)}) custom-call(bf16[8,128,128]{2,1,0:T(8,128)(2,1)} %get-tuple-element.6.first_ref, bf16[8,128,128]{2,1,0:T(8,128)(2,1)} %get-tuple-element.7.second_ref), custom_call_target="tpu_custom_call" | custom-call | bytes 1048576 | tf_op jit(solution)/shard_map/pallas_call | solution.py:606

commit v4 on v3

--- a/solution.py
+++ b/solution.py
@@ -101,67 +101,76 @@
 
 
 def totals_in_rows(totals):
-    return jnp.transpose(totals)[:8]
-
-
-def store_pieces(ref, sums, totals):
-    owners = ref.shape[0]
-    share = FEATURES // owners
-    for run in range(2):
-        ref[:, run * share : (run + 1) * share, :] = sums[run].reshape(owners, share, LANES)
-    ref[:, 2 * share :, :] = jnp.broadcast_to(totals_in_rows(totals)[None], (owners, 8, LANES))
+    return jnp.transpose(totals)[:4]
+
+
+def run_of(slot, groups):
+    second = jnp.where(slot >= groups, 1, 0)
+    group = slot - second * groups
+    odd = lax.rem(group, 2)
+    return (group - odd) * 2 + odd + second * 2
+
+
+def relation(own, others):
+    start_r, first_r, last_r = own
+    start, first, last = others
+    rising = (last == first_r) & (start < start_r)
+    falling = (first == last_r) & (start > start_r)
+    return jnp.where(rising, 1.0, 0.0), jnp.where(falling, 1.0, 0.0)
+
+
+def spans(ends, index, run_rows, length):
+    start = (index * run_rows).astype(F32)
+    found = (start, count_ends(ends, start), count_ends(ends, start + length - 1.0))
+    return tuple(jnp.broadcast_to(x, (index.shape[0], LANES)) for x in found)
+
+
+class Totals:
+    def __init__(self, ends, here, run_rows, groups, coef, ids_of):
+        self.groups, self.coef = groups, coef
+        slot = lax.broadcasted_iota(jnp.int32, (2 * groups, 1), 0)
+        others = spans(ends, run_of(slot, groups), run_rows, float(run_rows))
+        for run in range(2):
+            begin = ((here.first_run + 2 * run) * run_rows).astype(F32)
+            coef[2 * run], coef[2 * run + 1] = relation((begin, *ids_of(run)), others)
+
+    def collect(self, landed):
+        rows = []
+        sides = [jnp.concatenate([landed[:, side, :], landed[:, 2 + side, :]], axis=0) for side in range(2)]
+        for row in range(4):
+            rows.append(jnp.sum(self.coef[row] * sides[row % 2], axis=0, keepdims=True))
+        return jnp.transpose(jnp.concatenate(rows + [jnp.zeros((LANES - 4, LANES), F32)], axis=0))
 
 
 class Chain:
-    def __init__(self, ends, here, run_rows, inner, outer, row_coef, line_coef, own_coef, ids_of):
+    def __init__(self, ends, here, run_rows, inner, outer, row_coef, line_coef):
         self.inner, self.outer, self.share = inner, outer, FEATURES // inner
-        self.row_coef, self.line_coef, self.own_coef = row_coef, line_coef, own_coef
+        self.row_coef, self.line_coef = row_coef, line_coef
         runs = 2 * inner
         size = runs + outer
         slot = lax.broadcasted_iota(jnp.int32, (size, 1), 0)
         odd = jnp.where(lax.rem(slot, 4) >= 2, 1, 0)
         of_run = here.line * runs + slot + lax.rem(slot, 2) - odd
         index = jnp.where(slot < runs, of_run, (slot - runs) * runs)
-        start = (index * run_rows).astype(F32)
         length = jnp.where(slot < runs, run_rows, run_rows * runs).astype(F32)
-        first = jnp.broadcast_to(count_ends(ends, start), (size, LANES))
-        last = jnp.broadcast_to(count_ends(ends, start + length - 1.0), (size, LANES))
-        start = jnp.broadcast_to(start, (size, LANES))
+        others = spans(ends, index, run_rows, length)
+        start, first, last = others
         valid = jnp.broadcast_to(slot - runs, (size, LANES)) != here.line
         left = lanes_of(size) < HEAD_DIM
-
-        def relation(start_r, first_r, last_r):
-            rising = valid & (last == first_r) & (start < start_r)
-            falling = valid & (first == last_r) & (start > start_r)
-            return jnp.where(rising, 1.0, 0.0), jnp.where(falling, 1.0, 0.0)
-
         for run in range(runs):
-            at = slice(run, run + 1)
-            rising, falling = relation(start[at], first[at], last[at])
-            row_coef[run] = jnp.where(left, rising, falling)
-        for run in range(2):
-            begin = ((here.first_run + 2 * run) * run_rows).astype(F32)
-            own_coef[2 * run], own_coef[2 * run + 1] = relation(begin, *ids_of(run))
-        line_coef[0] = jnp.where(last == last[runs - 1 : runs], 1.0, 0.0)
-        line_coef[1] = jnp.where(first == first[:1], 1.0, 0.0)
-        line_coef[2] = jnp.where(left, line_coef[0], line_coef[1])
+            rising, falling = relation([x[run : run + 1] for x in others], others)
+            row_coef[run] = jnp.where(valid, jnp.where(left, rising, falling), 0.0)
+        ending = jnp.where(last == last[runs - 1 : runs], 1.0, 0.0)
+        line_coef[...] = jnp.where(left, ending, jnp.where(first == first[:1], 1.0, 0.0))
 
     def block(self, gathered, run):
         return gathered[run // 2, (run % 2) * self.share : (run % 2 + 1) * self.share, :]
 
-    def total(self, gathered, run, side):
-        row = 2 * self.share + 2 * (run % 2) + side
-        return gathered[run // 2, row : row + 1, :]
-
     def sum_line(self, gathered, out):
         found = jnp.zeros((self.share, LANES), F32)
-        totals = [jnp.zeros((1, LANES), F32)] * 2
         for run in range(2 * self.inner):
-            found = found + self.line_coef[2, run : run + 1, :] * self.block(gathered, run)
-            for side in range(2):
-                totals[side] = totals[side] + self.line_coef[side, run : run + 1, :] * self.total(gathered, run, side)
-        out[: self.share, :] = found
-        out[self.share :, :] = jnp.concatenate(totals + [jnp.zeros((6, LANES), F32)], axis=0)
+            found = found + self.line_coef[run : run + 1, :] * self.block(gathered, run)
+        out[...] = found
 
     def place(self, run):
         return run // 2, slice((run % 2) * self.share, (run % 2 + 1) * self.share)
@@ -179,7 +188,7 @@
 
     def from_lines(self, lines, out):
         runs = 2 * self.inner
-        blocks = [lines[line, : self.share, :] for line in range(self.outer)]
+        blocks = [lines[line] for line in range(self.outer)]
         for run in range(runs):
             owner, at = self.place(run)
             found = out[owner, at, :]
@@ -188,26 +197,17 @@
                 found = found + self.row_coef[run, source : source + 1, :] * blocks[line]
             out[owner, at, :] = found
 
-    def totals(self, gathered, lines):
-        runs = 2 * self.inner
-        rows = []
-        for row in range(4):
-            side = row % 2
-            found = jnp.zeros((1, LANES), F32)
-            for source in range(runs):
-                found = found + self.own_coef[row, source : source + 1, :] * self.total(gathered, source, side)
-            for line in range(self.outer):
-                at = self.share + side
-                found = found + self.own_coef[row, runs + line : runs + line + 1, :] * lines[line, at : at + 1, :]
-            rows.append(found)
-        return jnp.transpose(jnp.concatenate(rows + [jnp.zeros((LANES - 4, LANES), F32)], axis=0))
-
-    def states(self, state, totals):
-        result = []
-        for run in range(2):
-            sums = state[:, run * self.share : (run + 1) * self.share, :].reshape(FEATURES, LANES)
-            result.append(split2(beside(sums, totals)))
-        return result
+    def sums(self, state):
+        return [
+            state[:, run * self.share : (run + 1) * self.share, :].reshape(FEATURES, LANES) for run in range(2)
+        ]
+
+
+def store_pieces(ref, sums):
+    owners = ref.shape[0]
+    share = FEATURES // owners
+    for run in range(2):
+        ref[:, run * share : (run + 1) * share, :] = sums[run].reshape(owners, share, LANES)
 
 
 def over_peers(size, step):
@@ -233,6 +233,7 @@
         self.line = lax.div(self.wide, LINE)
         self.base = self.line * LINE
         self.inside = self.even - self.base + self.half
+        self.group = self.even + self.half
         self.first_run = 2 * self.even + self.half
 
     def of_member(self, member):
@@ -242,6 +243,10 @@
     def of_inside(self, inside):
         half = lax.rem(inside, 2)
         return {"wide": self.base + inside - half + self.second, "narrow": half * 4 + self.quarter}
+
+    def of_group(self, group):
+        half = lax.rem(group, 2)
+        return {"wide": group - half + self.second, "narrow": half * 4 + self.quarter}
 
     def of_line(self, line):
         return {"wide": self.wide - self.base + line * LINE, "narrow": self.narrow}
@@ -291,14 +296,15 @@
     q_ref, k_ref, v_ref, g_ref,
     kv_send, kv_ref, qg_send, qg_ref,
     piece, gathered, line, lines, moved, state, piece_g, gathered_g, line_g, lines_g, moved_g, state_g,
+    total_send, total_land, total_send_g, total_land_g,
     row_coef, line_coef, own_coef,
     done_q, back_q, done_k, back_k,
-    phi_k_ref, phi_q_ref, expo_k_ref, expo_q_ref, ids_ref, a_ref, total_ref,
+    phi_k_ref, phi_q_ref, expo_k_ref, expo_q_ref, ids_ref, a_ref, total_ref, inverse_ref,
     score_high, score_low, coupling_high, coupling_low, key_up_ref, value_up_ref,
     in_sem, send_sem, recv_sem,
 ):
     fine = kv_send.shape[0]
-    inner, outer = piece.shape[0], lines.shape[0]
+    inner, outer, coarse = piece.shape[0], lines.shape[0], total_land.shape[0]
     own = q_ref.shape[0]
     rows = own * fine
     run_rows = rows // 2
@@ -314,6 +320,9 @@
 
     def lengthwise(number, send, land):
         return Exchange(here.line, here.of_line, send, land, send_sem.at[number], recv_sem.at[number], True)
+
+    def everywhere(number, send, land):
+        return Exchange(here.group, here.of_group, send, land, send_sem.at[number], recv_sem.at[number], True)
 
     move_kv = within(0, kv_send, kv_ref)
     move_qg = within(1, qg_send, qg_ref)
@@ -325,6 +334,8 @@
     scatter_g = across(7, moved_g, state_g)
     give_q = within(8, done_q, back_q)
     give_k = within(9, done_k, back_k)
+    tell_s = everywhere(10, total_send, total_land)
+    tell_g = everywhere(11, total_send_g, total_land_g)
 
     barrier = pltpu.get_barrier_semaphore()
 
@@ -337,8 +348,7 @@
         over_peers(size, step)
 
     greet(here.member, here.of_member, fine)
-    greet(here.inside, here.of_inside, inner)
-    greet(here.line, here.of_line, outer)
+    greet(here.group, here.of_group, coarse)
     loads = [
         pltpu.make_async_copy(source, target, in_sem.at[i])
         for i, (source, target) in enumerate(
@@ -356,7 +366,7 @@
     loads[0].wait()
     loads[1].wait()
     pack(k_ref, v_ref, kv_send)
-    pl.semaphore_wait(barrier, fine + inner + outer - 3)
+    pl.semaphore_wait(barrier, fine + coarse - 2)
     move_kv.start()
     loads[2].wait()
     loads[3].wait()
@@ -412,19 +422,19 @@
         begin, end = run * run_rows, (run + 1) * run_rows
         return ids_ref[begin : begin + 1, :], ids_ref[end - 1 : end, :]
 
-    chain = Chain(ends, here, run_rows, inner, outer, row_coef, line_coef, own_coef, ids_of)
+    chain = Chain(ends, here, run_rows, inner, outer, row_coef, line_coef)
+    collector = Totals(ends, here, run_rows, coarse, own_coef, ids_of)
 
     def pieces_of(phi_ref, weights):
-        sums, totals = [], jnp.zeros((FEATURES, LANES), F32)
+        result = []
         for run in range(2):
             found = 0.0
             for strip, weight in zip(every, weights):
                 if strip.run == run:
                     for part in weight:
                         found = found + dot(phi_ref[strip.at, :], part, 0, 0)
-            sums.append(found[:, :LANES])
-            totals = totals + found[:, LANES:]
-        return sums, totals
+            result.append(found)
+        return result
 
     move_kv.arrived()
     weights = []
@@ -436,8 +446,11 @@
         front, back = strip.sides()
         vectors = packed[:, HEAD_DIM:].astype(F32)
         weights.append([beside(strip.pair(vectors, back, vectors, front), strip.line(back, front, ones)).astype(BF16)])
-    store_pieces(piece, *pieces_of(phi_k_ref, weights))
+    found = pieces_of(phi_k_ref, weights)
+    store_pieces(piece, [x[:, :LANES] for x in found])
     gather_s.start()
+    total_send[...] = totals_in_rows(found[0][:, LANES:] + found[1][:, LANES:])
+    tell_s.start()
 
     def values_of(run):
         packed = kv_ref[run * fine // 2 : (run + 1) * fine // 2].reshape(run_rows, LANES)
@@ -457,42 +470,69 @@
     chain.sum_line(gathered, line)
     share_s.start()
     chain.from_line(gathered, moved)
-    share_s.arrived()
-    chain.from_lines(lines, moved)
-    scatter_s.start()
-    totals = chain.totals(gathered, lines)
 
     for strip in every:
         total_ref[strip.at, :] = dot(score_high[strip.at, :], values[strip.run], 1, 0) + dot(
             score_low[strip.at, :], values[strip.run], 1, 0
         )
 
+    tell_s.arrived()
+    totals = collector.collect(total_land)
+    totals_high, totals_low = split2(totals)
+    weights = []
+    for strip in every:
+        front, back = strip.sides()
+        phi = phi_q_ref[strip.at, :]
+        grad = strip.of(qg_ref)[:, HEAD_DIM:].astype(F32)
+        far = dot(phi, totals_high, 1, 0) + dot(phi, totals_low, 1, 0)
+        lane = 2 * strip.run
+        denom = total_ref[strip.at, HEAD_DIM : HEAD_DIM + 1]
+        denom = denom + jnp.where(front[:, :1], far[:, lane : lane + 1], 0.0)
+        denom = denom + jnp.where(back[:, :1], far[:, lane + 1 : lane + 2], 0.0)
+        inverse = 1.0 / denom
+        inverse_ref[strip.at, :] = jnp.broadcast_to(inverse, (STRIP, LANES))
+        a = grad * inverse
+        a_ref[strip.at, :] = extended(a, jnp.zeros((STRIP, 1), F32))
+        weights.append(split2(strip.pair(a, back, a, front)))
+    store_pieces(piece_g, pieces_of(phi_q_ref, weights))
+    gather_g.start()
+
+    share_s.arrived()
+    chain.from_lines(lines, moved)
+    scatter_s.start()
+
+    for run in range(2):
+        whole = slice(run * run_rows, (run + 1) * run_rows)
+        a_high, a_low = split2(a_ref[whole, :])
+        both = dot(beside(a_high, a_low), score_high[whole, :], 0, 0)
+        value_up_ref[:, whole] = both[:LANES] + both[LANES:] + dot(a_high, score_low[whole, :], 0, 0)
+
+    gather_g.arrived()
+    chain.sum_line(gathered_g, line_g)
+    share_g.start()
+    chain.from_line(gathered_g, moved_g)
+
     scatter_s.arrived()
-    states = chain.states(state, totals)
+    states = [split2(beside(sums, totals)) for sums in chain.sums(state)]
     weights = []
     for strip in every:
         front, back = strip.sides()
         phi = phi_q_ref[strip.at, :]
         grad = strip.of(qg_ref)[:, HEAD_DIM:].astype(F32)
         high, low = states[strip.run]
-        far = dot(phi, high, 1, 0) + dot(phi, low, 1, 0)
-        total = total_ref[strip.at, :]
-        numer = total[:, :HEAD_DIM]
+        far = dot(phi, high[:, :LANES], 1, 0) + dot(phi, low[:, :LANES], 1, 0)
+        numer = total_ref[strip.at, :HEAD_DIM]
         numer = numer + jnp.where(front[:, :HEAD_DIM], far[:, :HEAD_DIM], 0.0)
-        numer = numer + jnp.where(back[:, :HEAD_DIM], far[:, HEAD_DIM:LANES], 0.0)
-        lane = LANES + 2 * strip.run
-        denom = total[:, HEAD_DIM : HEAD_DIM + 1]
-        denom = denom + jnp.where(front[:, :1], far[:, lane : lane + 1], 0.0)
-        denom = denom + jnp.where(back[:, :1], far[:, lane + 1 : lane + 2], 0.0)
-        inverse = 1.0 / denom
+        numer = numer + jnp.where(back[:, :HEAD_DIM], far[:, HEAD_DIM:], 0.0)
+        inverse = inverse_ref[strip.at, :HEAD_DIM]
         attended = numer * inverse
         total_ref[strip.at, :HEAD_DIM] = attended
-        bias = -jnp.sum(grad * attended, axis=1, keepdims=True) * inverse
-        a = grad * inverse
-        a_ref[strip.at, :] = extended(a, bias)
-        weights.append(split2(beside(strip.pair(a, back, a, front), strip.line(back, front, bias))))
-    store_pieces(piece_g, *pieces_of(phi_q_ref, weights))
-    gather_g.start()
+        bias = -jnp.sum(grad * attended, axis=1, keepdims=True) * inverse[:, :1]
+        a_ref[strip.at, :] = extended(a_ref[strip.at, :HEAD_DIM], bias)
+        weights.append(split2(strip.line(back, front, bias)))
+    found = pieces_of(phi_q_ref, weights)
+    total_send_g[...] = totals_in_rows(found[0] + found[1])
+    tell_g.start()
 
     def query_part(strip):
         front, back = strip.sides()
@@ -515,29 +555,23 @@
     for strip in every[: strips // 2]:
         query_part(strip)
 
-    gather_g.arrived()
-    chain.sum_line(gathered_g, line_g)
-    share_g.start()
-    chain.from_line(gathered_g, moved_g)
-    for strip in every[strips // 2 :]:
-        query_part(strip)
     share_g.arrived()
     chain.from_lines(lines_g, moved_g)
     scatter_g.start()
+
+    for strip in every[strips // 2 :]:
+        query_part(strip)
     give_q.start()
-    totals = chain.totals(gathered_g, lines_g)
 
     for run in range(2):
         whole = slice(run * run_rows, (run + 1) * run_rows)
-        a_high, a_low = split2(a_ref[whole, :])
-        high = score_high[whole, :]
-        both = dot(beside(a_high, a_low), high, 0, 0)
-        value_up_ref[:, whole] = both[:LANES] + both[LANES:] + dot(a_high, score_low[whole, :], 0, 0)
         phi = phi_q_ref[whole, :]
         key_up_ref[:, whole] = dot(phi, coupling_high[whole, :], 0, 0) + dot(phi, coupling_low[whole, :], 0, 0)
 
     scatter_g.arrived()
-    states_g = chain.states(state_g, totals)
+    tell_g.arrived()
+    totals_g = collector.collect(total_land_g)
+    states_g = [split2(beside(sums, totals_g)) for sums in chain.sums(state_g)]
     for strip in every:
         front, back = strip.sides()
         phi = phi_k_ref[strip.at, :]
@@ -559,7 +593,7 @@
     give_k.arrived()
     second_ref[...] = back_k[...]
     for each in (
-        move_kv, move_qg, gather_s, share_s, scatter_s, gather_g, share_g, scatter_g, give_q, give_k
+        move_kv, move_qg, gather_s, share_s, scatter_s, gather_g, share_g, scatter_g, give_q, give_k, tell_s, tell_g
     ):
         each.sent()
 
@@ -576,19 +610,19 @@
     anywhere = pl.BlockSpec(memory_space=pl.ANY)
     tokens = pltpu.VMEM(query_rows.shape, BF16)
     blocks = pltpu.VMEM((fine, own, LANES), BF16)
-    pieces = pltpu.VMEM((LINE, 2 * share + 8, LANES), F32)
+    pieces = pltpu.VMEM((LINE, 2 * share, LANES), F32)
     results = pltpu.VMEM((LINE, 2 * share, LANES), F32)
-    line_rows = share + 8
-    lines = [pltpu.VMEM((line_rows, LANES), F32), pltpu.VMEM((outer, line_rows, LANES), F32)]
+    lines = [pltpu.VMEM((share, LANES), F32), pltpu.VMEM((outer, share, LANES), F32)]
+    told = [pltpu.VMEM((4, LANES), F32), pltpu.VMEM((coarse, 4, LANES), F32)]
     phase = [pieces] * 2 + lines + [results] * 2
-    coefs = [pltpu.VMEM((count, sources, LANES), F32) for count in (2 * LINE, 3, 4)]
+    coefs = [pltpu.VMEM(x + (LANES,), F32) for x in ((2 * LINE, sources), (sources,), (4, 2 * coarse))]
     narrow_rows = pltpu.VMEM((rows, LANES), BF16)
     wide_rows = pltpu.VMEM((rows, LANES), F32)
     square = pltpu.VMEM((rows, rows // 2), BF16)
     turned = pltpu.VMEM((LANES, rows), F32)
-    scratch = [tokens] * 4 + [blocks] * 4 + phase * 2 + coefs + [blocks] * 4
-    scratch += [narrow_rows] * 2 + [wide_rows] * 5 + [square] * 4 + [turned] * 2
-    scratch += [pltpu.SemaphoreType.DMA((count,)) for count in (4, 10, 10)]
+    scratch = [tokens] * 4 + [blocks] * 4 + phase * 2 + told * 2 + coefs + [blocks] * 4
+    scratch += [narrow_rows] * 2 + [wide_rows] * 6 + [square] * 4 + [turned] * 2
+    scratch += [pltpu.SemaphoreType.DMA((count,)) for count in (4, 12, 12)]
     first, second = pl.pallas_call(
         main_kernel,
         out_shape=(packed, packed),

time: 77.4 us -> 71 us (0.917)
  Pallas kernels: 76.5 us -> 70.1 us
    pallas_call x1, Pallas kernels: 74.6 us -> 68.1 us  [body(): pl.pallas_call(main_kernel, out_shape=(packed, packed), in_specs=[anywher...]
where the time goes in v4:
time: 71 us; the launch traced here: 70.8 us
  Pallas kernels  70.1 us (99%)
    pallas_call x1, Pallas kernels, body(): pl.pallas_call(main_kernel, out_shape=(packed, packed), in_specs=[anywher...  68.1 us
    pallas_call x1, Pallas kernels, body(): pl.pallas_call(unpack_kernel, out_shape=(out, out, out, out), in_specs=[v...  1.99 us

profile of v4, /device:TPU:1, one launch (start us, length us, event | category | flops | bytes accessed | tf_op | source)
XLA Modules:
  0.0 70.8 jit_solution(4003141734397938993)
XLA Ops:
  0.6 68.1 %shard_map.93 = (bf16[8,128,128]{2,1,0:T(8,128)(2,1)}, bf16[8,128,128]{2,1,0:T(8,128)(2,1)}) custom-call(bf16[128,512]{1,0:T(8,128)(2,1)} %q_any.1, bf16[128,512]{1,0:T(8,128)(2,1)} %k_any.1, bf16[128,512]{1,0:T(8,128)(2,1)} %v_any.1, bf16[128,512]{1,0:T(8,128)(2,1)} %g_any.1, s32[8,128]{1,0:T(8,128)} %bitcast.3, f32[64,128]{1,0:T(8,128)} %bitcast.2), custom_call_target="tpu_custom_call" | custom-call | flops 1610612736 | bytes 1048576 | tf_op jit(solution)/shard_map/pallas_call | solution.py:626
  68.8 2.0 %shard_map.94 = (bf16[128,512]{1,0:T(8,128)(2,1)}, bf16[128,512]{1,0:T(8,128)(2,1)}, bf16[128,512]{1,0:T(8,128)(2,1)}, bf16[128,512]{1,0:T(8,128)(2,1)}) custom-call(bf16[8,128,128]{2,1,0:T(8,128)(2,1)} %get-tuple-element.6.first_ref, bf16[8,128,128]{2,1,0:T(8,128)(2,1)} %get-tuple-element.7.second_ref), custom_call_target="tpu_custom_call" | custom-call | bytes 1048576 | tf_op jit(solution)/shard_map/pallas_call | solution.py:640

commit v5 on v4

--- a/solution.py
+++ b/solution.py
@@ -301,7 +301,7 @@
     done_q, back_q, done_k, back_k,
     phi_k_ref, phi_q_ref, expo_k_ref, expo_q_ref, ids_ref, a_ref, total_ref, inverse_ref,
     score_high, score_low, coupling_high, coupling_low, key_up_ref, value_up_ref,
-    in_sem, send_sem, recv_sem,
+    in_sem, send_sem, recv_sem, line_sem,
 ):
     fine = kv_send.shape[0]
     inner, outer, coarse = piece.shape[0], lines.shape[0], total_land.shape[0]
@@ -339,16 +339,14 @@
 
     barrier = pltpu.get_barrier_semaphore()
 
-    def greet(me, device_of, size):
+    def greet(sem, me, device_of, size):
         def step(offset):
             pl.semaphore_signal(
-                barrier, inc=1, device_id=device_of(lax.rem(me + offset, size)), device_id_type=MESH
+                sem, inc=1, device_id=device_of(lax.rem(me + offset, size)), device_id_type=MESH
             )
 
         over_peers(size, step)
 
-    greet(here.member, here.of_member, fine)
-    greet(here.group, here.of_group, coarse)
     loads = [
         pltpu.make_async_copy(source, target, in_sem.at[i])
         for i, (source, target) in enumerate(
@@ -357,6 +355,9 @@
     ]
     for load in loads:
         load.start()
+    greet(barrier, here.member, here.of_member, fine)
+    greet(barrier, here.inside, here.of_inside, inner)
+    greet(barrier, here.line, here.of_line, outer)
 
     def pack(left, right, target):
         for head in range(fine):
@@ -366,8 +367,9 @@
     loads[0].wait()
     loads[1].wait()
     pack(k_ref, v_ref, kv_send)
-    pl.semaphore_wait(barrier, fine + coarse - 2)
+    pl.semaphore_wait(barrier, fine + inner + outer - 3)
     move_kv.start()
+    greet(line_sem, here.line, here.of_line, outer)
     loads[2].wait()
     loads[3].wait()
     pack(q_ref, g_ref, qg_send)
@@ -450,6 +452,7 @@
     store_pieces(piece, [x[:, :LANES] for x in found])
     gather_s.start()
     total_send[...] = totals_in_rows(found[0][:, LANES:] + found[1][:, LANES:])
+    pl.semaphore_wait(line_sem, outer - 1)
     tell_s.start()
 
     def values_of(run):
@@ -623,6 +626,7 @@
     scratch = [tokens] * 4 + [blocks] * 4 + phase * 2 + told * 2 + coefs + [blocks] * 4
     scratch += [narrow_rows] * 2 + [wide_rows] * 6 + [square] * 4 + [turned] * 2
     scratch += [pltpu.SemaphoreType.DMA((count,)) for count in (4, 12, 12)]
+    scratch += [pltpu.SemaphoreType.REGULAR]
     first, second = pl.pallas_call(
         main_kernel,
         out_shape=(packed, packed),

time: 71 us -> 68.6 us (0.966)
  Pallas kernels: 70.1 us -> 67.7 us
    pallas_call x1, Pallas kernels: 68.1 us -> 65.7 us  [body(): pl.pallas_call(main_kernel, out_shape=(packed, packed), in_specs=[anywher...]
where the time goes in v5:
time: 68.6 us; the launch traced here: 68.4 us
  Pallas kernels  67.7 us (99%)
    pallas_call x1, Pallas kernels, body(): pl.pallas_call(main_kernel, out_shape=(packed, packed), in_specs=[anywher...  65.7 us
    pallas_call x1, Pallas kernels, body(): pl.pallas_call(unpack_kernel, out_shape=(out, out, out, out), in_specs=[v...  1.99 us

profile of v5, /device:TPU:1, one launch (start us, length us, event | category | flops | bytes accessed | tf_op | source)
XLA Modules:
  0.0 68.4 jit_solution(4086523920289565382)
XLA Ops:
  0.6 65.7 %shard_map.93 = (bf16[8,128,128]{2,1,0:T(8,128)(2,1)}, bf16[8,128,128]{2,1,0:T(8,128)(2,1)}) custom-call(bf16[128,512]{1,0:T(8,128)(2,1)} %q_any.1, bf16[128,512]{1,0:T(8,128)(2,1)} %k_any.1, bf16[128,512]{1,0:T(8,128)(2,1)} %v_any.1, bf16[128,512]{1,0:T(8,128)(2,1)} %g_any.1, s32[8,128]{1,0:T(8,128)} %bitcast.3, f32[64,128]{1,0:T(8,128)} %bitcast.2), custom_call_target="tpu_custom_call" | custom-call | flops 1610612736 | bytes 1048576 | tf_op jit(solution)/shard_map/pallas_call | solution.py:630
  66.4 2.0 %shard_map.94 = (bf16[128,512]{1,0:T(8,128)(2,1)}, bf16[128,512]{1,0:T(8,128)(2,1)}, bf16[128,512]{1,0:T(8,128)(2,1)}, bf16[128,512]{1,0:T(8,128)(2,1)}) custom-call(bf16[8,128,128]{2,1,0:T(8,128)(2,1)} %get-tuple-element.6.first_ref, bf16[8,128,128]{2,1,0:T(8,128)(2,1)} %get-tuple-element.7.second_ref), custom_call_target="tpu_custom_call" | custom-call | bytes 1048576 | tf_op jit(solution)/shard_map/pallas_call | solution.py:644

commit v6 on v5

--- a/solution.py
+++ b/solution.py
@@ -508,7 +508,9 @@
         whole = slice(run * run_rows, (run + 1) * run_rows)
         a_high, a_low = split2(a_ref[whole, :])
         both = dot(beside(a_high, a_low), score_high[whole, :], 0, 0)
-        value_up_ref[:, whole] = both[:LANES] + both[LANES:] + dot(a_high, score_low[whole, :], 0, 0)
+        value_up_ref[whole, :] = jnp.transpose(
+            both[:LANES] + both[LANES:] + dot(a_high, score_low[whole, :], 0, 0)
+        )
 
     gather_g.arrived()
     chain.sum_line(gathered_g, line_g)
@@ -569,26 +571,34 @@
     for run in range(2):
         whole = slice(run * run_rows, (run + 1) * run_rows)
         phi = phi_q_ref[whole, :]
-        key_up_ref[:, whole] = dot(phi, coupling_high[whole, :], 0, 0) + dot(phi, coupling_low[whole, :], 0, 0)
+        key_up_ref[whole, :] = jnp.transpose(
+            dot(phi, coupling_high[whole, :], 0, 0) + dot(phi, coupling_low[whole, :], 0, 0)
+        )
 
     scatter_g.arrived()
+    sums_g = chain.sums(state_g)
+    for strip in every:
+        front, back = strip.sides()
+        phi = phi_k_ref[strip.at, :]
+        high, low = split2(sums_g[strip.run])
+        far = dot(phi, high, 1, 0) + dot(phi, low, 1, 0)
+        total = value_up_ref[strip.at, :HEAD_DIM]
+        total = total + jnp.where(front[:, :HEAD_DIM], far[:, :HEAD_DIM], 0.0)
+        value_up_ref[strip.at, :HEAD_DIM] = total + jnp.where(back[:, :HEAD_DIM], far[:, HEAD_DIM:], 0.0)
+
     tell_g.arrived()
     totals_g = collector.collect(total_land_g)
-    states_g = [split2(beside(sums, totals_g)) for sums in chain.sums(state_g)]
+    states_g = [split2(beside(sums, totals_g)) for sums in sums_g]
     for strip in every:
         front, back = strip.sides()
-        phi = phi_k_ref[strip.at, :]
         packed = strip.of(kv_ref)
         vectors = packed[:, HEAD_DIM:].astype(F32)
         use = beside(strip.pair(vectors, front, vectors, back), strip.line(front, back, ones)).astype(BF16)
         high, low = states_g[strip.run]
-        up = jnp.transpose(key_up_ref[:, strip.at]) + dot(use, high, 1, 1) + dot(use, low, 1, 1)
-        far = dot(phi, high[:, :LANES], 1, 0) + dot(phi, low[:, :LANES], 1, 0)
-        total = jnp.transpose(value_up_ref[:, strip.at])[:, :HEAD_DIM]
-        total = total + jnp.where(front[:, :HEAD_DIM], far[:, :HEAD_DIM], 0.0)
-        total = total + jnp.where(back[:, :HEAD_DIM], far[:, HEAD_DIM:], 0.0)
+        up = key_up_ref[strip.at, :] + dot(use, high, 1, 1) + dot(use, low, 1, 1)
         key_grad = feature_grad(packed[:, :HEAD_DIM], expo_k_ref[strip.at, :], up, grad_parts)
-        done_k[strip.slots] = beside(key_grad, total).astype(BF16).reshape(blocks, own, LANES)
+        done = beside(key_grad, value_up_ref[strip.at, :HEAD_DIM]).astype(BF16)
+        done_k[strip.slots] = done.reshape(blocks, own, LANES)
     give_k.start()
 
     give_q.arrived()
@@ -622,9 +632,8 @@
     narrow_rows = pltpu.VMEM((rows, LANES), BF16)
     wide_rows = pltpu.VMEM((rows, LANES), F32)
     square = pltpu.VMEM((rows, rows // 2), BF16)
-    turned = pltpu.VMEM((LANES, rows), F32)
     scratch = [tokens] * 4 + [blocks] * 4 + phase * 2 + told * 2 + coefs + [blocks] * 4
-    scratch += [narrow_rows] * 2 + [wide_rows] * 6 + [square] * 4 + [turned] * 2
+    scratch += [narrow_rows] * 2 + [wide_rows] * 6 + [square] * 4 + [wide_rows] * 2
     scratch += [pltpu.SemaphoreType.DMA((count,)) for count in (4, 12, 12)]
     scratch += [pltpu.SemaphoreType.REGULAR]
     first, second = pl.pallas_call(

time: 68.6 us -> 68.8 us (level)
  no operation moved by 1% of the time
where the time goes in v6:
time: 68.8 us; the launch traced here: 68.5 us
  Pallas kernels  67.9 us (99%)
    pallas_call x1, Pallas kernels, body(): pl.pallas_call(main_kernel, out_shape=(packed, packed), in_specs=[anywher...  65.9 us
    pallas_call x1, Pallas kernels, body(): pl.pallas_call(unpack_kernel, out_shape=(out, out, out, out), in_specs=[v...  1.99 us

profile of v6, /device:TPU:1, one launch (start us, length us, event | category | flops | bytes accessed | tf_op | source)
XLA Modules:
  0.0 68.5 jit_solution(14833144750616702672)
XLA Ops:
  0.6 65.9 %shard_map.93 = (bf16[8,128,128]{2,1,0:T(8,128)(2,1)}, bf16[8,128,128]{2,1,0:T(8,128)(2,1)}) custom-call(bf16[128,512]{1,0:T(8,128)(2,1)} %q_any.1, bf16[128,512]{1,0:T(8,128)(2,1)} %k_any.1, bf16[128,512]{1,0:T(8,128)(2,1)} %v_any.1, bf16[128,512]{1,0:T(8,128)(2,1)} %g_any.1, s32[8,128]{1,0:T(8,128)} %bitcast.3, f32[64,128]{1,0:T(8,128)} %bitcast.2), custom_call_target="tpu_custom_call" | custom-call | flops 1610612736 | bytes 1048576 | tf_op jit(solution)/shard_map/pallas_call | solution.py:639
  66.5 2.0 %shard_map.94 = (bf16[128,512]{1,0:T(8,128)(2,1)}, bf16[128,512]{1,0:T(8,128)(2,1)}, bf16[128,512]{1,0:T(8,128)(2,1)}, bf16[128,512]{1,0:T(8,128)(2,1)}) custom-call(bf16[8,128,128]{2,1,0:T(8,128)(2,1)} %get-tuple-element.6.first_ref, bf16[8,128,128]{2,1,0:T(8,128)(2,1)} %get-tuple-element.7.second_ref), custom_call_target="tpu_custom_call" | custom-call | bytes 1048576 | tf_op jit(solution)/shard_map/pallas_call | solution.py:653
